TPU v7x, 128 devices: a whole 4x4x4 slice. The times are simulated.
128 devices in a mesh: dp: 2 (over core), ctx: 16 (over y, z), tp: 4 (over x).
Axes of the slice: x: 4, y: 4, z: 4, core: 2. Of those that a mesh axis runs over, the one named last changes fastest.
Arguments:
- response: bfloat16 [32, 512, 4096], P(('dp', 'ctx'), None, 'tp'), parts along dimension 0, may hold values from -6 to 6
- owner: int32 [2], P('dp'), parts along dimension 0, may hold values from 0 to 15, as said below
- doc_lengths: int32 [32], P(('dp', 'ctx')), parts along dimension 0, may hold values from 512 to 2048, as said below
- doc_keys: bfloat16 [65536, 8, 128], P(('dp', 'ctx'), 'tp'), parts along dimension 0, may hold values from -2000 to 2000
- doc_values: bfloat16 [65536, 8, 128], P(('dp', 'ctx'), 'tp'), parts along dimension 0, may hold values from -6 to 6
- w_query: bfloat16 [4096, 4096], P(None, 'tp'), may hold values from -0.09375 to 0.09375
- w_key: bfloat16 [4096, 1024], P(None, 'tp'), may hold values from -0.375 to 0.375
- w_value: bfloat16 [4096, 1024], P(None, 'tp'), may hold values from -0.09375 to 0.09375
- w_out: bfloat16 [4096, 4096], P('tp'), may hold values from -0.09375 to 0.09375
Outputs:
- layer_out: bfloat16 [1024, 4096], P(('dp', 'ctx'), 'tp'), parts along dimension 0
There are 2 independent parts, one for each index of `dp`. A program takes and returns all parts, laid end to end along the dimension named above; an argument that names none is the same for every part. Nothing has to cross between parts.
Inputs may be any that keep to these rules, and one draw needn't show every extreme that they name: The first part's owner lies in the lower half of ctx's indices; the second part's owner is the last index, 15. `doc_lengths`: some index of ctx has a full cache in every draw.
All inputs are finite; a program needn't handle non-finite values.
Results may differ from a plain program's by a relative error of at most 0.014.
The roundings to bfloat16 on the way count: a program that leaves them out, or rounds other values in their place, can miss the bound.
Values may be sent and summed in bfloat16 or wider, within the bound.
No kernel may reach another device: no remote copies, remote signals or barrier semaphores. Data moves between devices by JAX's collectives and lax.ppermute only.
A program may use at most 192 MiB of HBM per device.

v0:
```python
import jax
import jax.numpy as jnp
from jax import lax
from jax.sharding import PartitionSpec as P

masked_score = -1e30


def spread(shard, axis, root):
    mine = lax.axis_index(axis) == root
    return lax.psum(jnp.where(mine, shard, jnp.zeros_like(shard)), axis)


def joined(value, axis, join):
    pieces = jax.tree.map(lambda part: lax.all_gather(part, axis), value)
    head = jax.tree.map(lambda part: part[0], pieces)
    tail = jax.tree.map(lambda part: part[1:], pieces)
    running, _ = lax.scan(lambda running, section: (join(running, section), None), head, tail)
    return running


def attend(queries, key_block, value_block, visible, group_size):
    kv_count = key_block.shape[1]
    row_count = queries.shape[0]
    head_dim = key_block.shape[2]
    query_heads = queries.reshape(row_count, kv_count, group_size, head_dim)
    maxima, totals, weighted = ([], [], [])
    for kv_head in range(kv_count):
        scores = jnp.einsum(
            "rgd,kd->rgk",
            query_heads[:, kv_head],
            key_block[:, kv_head],
            preferred_element_type=jnp.float32,
        ) * head_dim ** (-0.5)
        scores = jnp.where(visible[:, None, :], scores, masked_score)
        row_max = jnp.max(scores, -1)
        expos = jnp.exp(scores - row_max[..., None])
        maxima.append(row_max)
        totals.append(jnp.sum(expos, -1))
        weighted.append(
            jnp.einsum(
                "rgk,kd->rgd",
                expos.astype(jnp.bfloat16),
                value_block[:, kv_head],
                preferred_element_type=jnp.float32,
            )
        )
    return (jnp.concatenate(maxima, 1), jnp.concatenate(totals, 1), jnp.concatenate(weighted, 1))


def combine(first, second):
    row_max = jnp.maximum(first[0], second[0])
    first_scale = jnp.exp(first[0] - row_max)
    second_scale = jnp.exp(second[0] - row_max)
    return (
        row_max,
        first[1] * first_scale + second[1] * second_scale,
        first[2] * first_scale[..., None] + second[2] * second_scale[..., None],
    )


def local(response, owner, doc_lengths, doc_keys, doc_values, w_query, w_key, w_value, w_out):
    root = owner[0]
    is_owner = lax.axis_index("ctx") == root
    row_count = response.shape[1]
    head_dim = doc_keys.shape[2]
    kv_local = doc_keys.shape[1]
    heads_local = w_query.shape[1] // head_dim
    group_size = heads_local // kv_local
    cache_rows = doc_keys.shape[0]
    visible = jnp.arange(cache_rows) < doc_lengths[0]
    doc_visible = jnp.broadcast_to(visible[None, :], (row_count, cache_rows))
    causal = lax.broadcasted_iota(jnp.int32, (row_count, row_count), 1) <= lax.broadcasted_iota(
        jnp.int32, (row_count, row_count), 0
    )

    def self_partial(hidden_rows, queries):
        self_keys = (
            jnp.dot(hidden_rows, w_key, preferred_element_type=jnp.float32)
            .astype(jnp.bfloat16)
            .reshape(row_count, kv_local, head_dim)
        )
        self_values = (
            jnp.dot(hidden_rows, w_value, preferred_element_type=jnp.float32)
            .astype(jnp.bfloat16)
            .reshape(row_count, kv_local, head_dim)
        )
        return attend(queries, self_keys, self_values, causal, group_size)

    def no_partial(hidden_rows, queries):
        return (
            jnp.full((row_count, heads_local), masked_score, jnp.float32),
            jnp.zeros((row_count, heads_local), jnp.float32),
            jnp.zeros((row_count, heads_local, head_dim), jnp.float32),
        )

    hidden_rows = spread(response[0], "ctx", root)
    hidden_rows = lax.all_gather(hidden_rows, "tp", axis=1, tiled=True)
    queries = jnp.dot(hidden_rows, w_query, preferred_element_type=jnp.float32).astype(jnp.bfloat16)
    own_part = lax.cond(is_owner, self_partial, no_partial, hidden_rows, queries)
    doc_part = attend(queries, doc_keys, doc_values, doc_visible, group_size)
    local_part = combine(doc_part, own_part)
    share = row_count // lax.axis_size("ctx")
    row_max, totals, weighted = joined(local_part, "ctx", combine)
    start = lax.axis_index("ctx") * share
    totals = lax.dynamic_slice_in_dim(totals, start, share, 0)
    weighted = lax.dynamic_slice_in_dim(weighted, start, share, 0)
    attended = (
        (weighted / totals[..., None]).astype(jnp.bfloat16).reshape(share, heads_local * head_dim)
    )
    partial_out = jnp.dot(attended, w_out, preferred_element_type=jnp.float32)
    return lax.psum_scatter(partial_out, "tp", scatter_dimension=1, tiled=True).astype(jnp.bfloat16)


def solution(mesh):
    placed = (
        P(("dp", "ctx"), None, "tp"),
        P("dp"),
        P(("dp", "ctx")),
        P(("dp", "ctx"), "tp", None),
        P(("dp", "ctx"), "tp", None),
        P(None, "tp"),
        P(None, "tp"),
        P(None, "tp"),
        P("tp", None),
    )
    return jax.shard_map(
        local, mesh=mesh, in_specs=placed, out_specs=P(("dp", "ctx"), "tp"), check_vma=False
    )
```

profile of v0, /device:TPU:0, one launch (start us, length us, event | category | flops | bytes accessed | tf_op | source)
XLA Modules:
  0.0 594.4 jit_solution(11110573585050779744)
XLA Ops:
  7.3 1.1 select_bitcast_fusion
  8.4 91.8 %all-reduce.2.cloned.1.call-done = bf16[512,1024]{1,0:T(8,128)(2,1)} async-done(((bf16[512,1024]{1,0:T(8,128)(2,1)}), bf16[512,1024]{1,0:T(8,128)(2,1)}) %all-reduce.2.cloned.1.call-update) | async-done | bytes 1048592 | tf_op jit(solution)/shard_map/psum | solution.py:11
  101.0 2.5 fusion.49
  103.5 2.4 fusion.47
  105.9 43.4 %all-gather.6.cloned.1.call-done = bf16[512,4096]{1,0:T(8,128)(2,1)} async-done(((bf16[512,1024]{1,0:T(8,128)(2,1)}), bf16[512,4096]{1,0:T(8,128)(2,1)}) %all-gather.6.cloned.1.call-update) | async-done | bytes 4194320 | tf_op jit(solution)/shard_map/all_gather | solution.py:98
  149.3 9.1 %convolution_convert_fusion.2 = bf16[512,1024]{1,0:T(8,128)(2,1)S(1)} fusion(bf16[512,4096]{1,0:T(8,128)(2,1)} %all-gather.6.cloned.1.call-done, bf16[4096,1024]{1,0:T(8,128)(2,1)} %param.18), kind=kOutput, calls=%fused_computation.57 | convolution fusion | flops 4295491584 | bytes 13631488 | tf_op jit(solution)/shard_map/dot_general | solution.py:99
  158.5 0.8 reshape.28
  159.2 1.1 fusion.48
  160.4 4.8 fusion.22
  165.2 11.6 %fusion.25 = (f32[512,4]{0,1:T(4,128)}, f32[512,4]{0,1:T(4,128)S(1)}, f32[512,4,2048]{2,0,1:T(8,128)}) fusion(f32[512,4,2048]{2,0,1:T(8,128)S(1)} %get-tuple-element.152, f32[512,4]{0,1:T(4,128)} %get-tuple-element.151, pred[2048]{0:T(1024)(128)(4,1)S(1)} %iota_compare_fusion, bf16[2048,1,128]{2,1,0:T(2,128)(2,1)} %get-tuple-element.148, ...), kind=kOutput, calls=%fused_computation.48 | convolution fusion | flops 1103097856 | bytes 34629632 | tf_op jit(solution)/shard_map/rgd,kd->rgk/dot_general | solution.py:29
  176.8 8.4 %fusion.27 = f32[512,4]{0,1:T(4,128)} fusion(f32[512,4,2048]{2,0,1:T(8,128)} %get-tuple-element.153, f32[512,4]{0,1:T(4,128)S(1)} %get-tuple-element.116, pred[2048]{0:T(1024)(128)(4,1)S(1)} %iota_compare_fusion), kind=kLoop, calls=%fused_computation.50 | loop fusion | flops 16775168 | bytes 16795648 | tf_op jit(solution)/shard_map/reduce_sum | solution.py:39
  185.3 10.3 %fusion.28 = f32[512,4,128]{2,0,1:T(8,128)} fusion(f32[512,4,2048]{2,0,1:T(8,128)} %get-tuple-element.153, f32[512,4]{0,1:T(4,128)S(1)} %get-tuple-element.116, pred[2048]{0:T(1024)(128)(4,1)S(1)} %iota_compare_fusion, bf16[2048,1,128]{2,1,0:T(2,128)(2,1)S(1)} %copy-done.4), kind=kOutput, calls=%fused_computation.51 | convolution fusion | flops 1090519040 | bytes 18360320 | tf_op jit(solution)/shard_map/rgk,kd->rgd/dot_general | solution.py:41
  195.6 4.5 fusion.30
  200.4 1.5 conditional.1
  200.4 1.5 broadcast.34
  202.0 3.8 fusion.34
  205.8 37.5 %all-gather = f32[8192,8]{0,1:T(8,128)S(1)} all-gather(f32[512,8]{0,1:T(8,128)S(1)} %get-tuple-element.150), channel_id=2, replica_groups=mesh['dp'=2,'ctx'=16,'tp'=4] {'ctx'}, dimensions={0}, use_global_device_ids=true | all-gather | bytes 278528 | tf_op jit(solution)/shard_map/all_gather | solution.py:15
  243.3 21.2 %all-gather.1 = f32[8192,8]{0,1:T(8,128)S(1)} all-gather(f32[512,8]{0,1:T(8,128)S(1)} %get-tuple-element.135), channel_id=3, replica_groups=mesh['dp'=2,'ctx'=16,'tp'=4] {'ctx'}, dimensions={0}, use_global_device_ids=true | all-gather | bytes 278528 | tf_op jit(solution)/shard_map/all_gather | solution.py:15
  264.6 154.3 %all-gather.8.cloned.1.call-done = f32[8192,8,128]{2,0,1:T(8,128)} async-done(((f32[512,8,128]{2,0,1:T(8,128)}), f32[8192,8,128]{2,0,1:T(8,128)}) %all-gather.8.cloned.1.call-update) | async-done | bytes 33554448 | tf_op jit(solution)/shard_map/all_gather | solution.py:15
  418.9 1.6 slice-done
  420.5 1.2 copy.68
  421.7 21.6 %slice.85 = f32[7680,8,128]{2,0,1:T(8,128)} slice(f32[8192,8,128]{2,0,1:T(8,128)} %all-gather.8.cloned.1.call-done), slice={[512:8192], [0:8], [0:128]} | slice | bytes 62914560 | tf_op jit(solution)/shard_map/slice | solution.py:17
  443.3 115.9 %while.14 = (s32[]{:T(128)}, f32[512,8]{0,1:T(8,128)S(1)}, f32[512,8]{0,1:T(8,128)S(1)}, f32[512,8,128]{2,1,0:T(8,128)S(1)}, f32[15,512,8]{1,2,0:T(8,128)S(1)}, ...) while((s32[]{:T(128)}, f32[512,8]{0,1:T(8,128)S(1)}, f32[512,8]{0,1:T(8,128)S(1)}, ...), condition=%wide.region_12.13_spmd, body=%wide.region_11.12_spmd.sunk | while | flops 1597442 | bytes 10715229 | solution.py:18
  443.4 0.1 copy.121
  443.6 1.7 constant_dynamic-slice_fusion.3
  445.3 5.7 fusion.60
  451.2 0.1 copy.121
  451.3 1.7 constant_dynamic-slice_fusion.3
  453.1 5.7 fusion.60
  458.9 0.1 copy.121
  459.0 1.7 constant_dynamic-slice_fusion.3
  460.8 5.7 fusion.60
  466.6 0.1 copy.121
  466.8 1.7 constant_dynamic-slice_fusion.3
  468.5 5.7 fusion.60
  474.3 0.1 copy.121
  474.5 1.7 constant_dynamic-slice_fusion.3
  476.2 5.7 fusion.60
  482.1 0.1 copy.121
  482.2 1.7 constant_dynamic-slice_fusion.3
  484.0 5.7 fusion.60
  489.8 0.1 copy.121
  489.9 1.7 constant_dynamic-slice_fusion.3
  491.7 5.7 fusion.60
  497.5 0.1 copy.121
  497.7 1.7 constant_dynamic-slice_fusion.3
  499.4 5.7 fusion.60
  505.4 1.7 constant_dynamic-slice_fusion.3
  507.1 5.7 fusion.60
  513.1 1.7 constant_dynamic-slice_fusion.3
  514.9 5.7 fusion.60
  520.8 1.7 constant_dynamic-slice_fusion.3
  522.6 5.7 fusion.60
  528.6 1.7 constant_dynamic-slice_fusion.3
  530.3 5.7 fusion.60
  536.3 1.7 constant_dynamic-slice_fusion.3
  538.1 5.7 fusion.60
  544.0 1.7 constant_dynamic-slice_fusion.3
  545.8 5.7 fusion.60
  551.8 1.7 constant_dynamic-slice_fusion.3
  553.5 5.7 fusion.60
  559.5 5.7 fusion.37
  565.2 21.1 %reduce-scatter.2.cloned.1.call-done = f32[32,1024]{1,0:T(8,128)} async-done(((f32[32,4096]{1,0:T(8,128)}), f32[32,1024]{1,0:T(8,128)}) %reduce-scatter.2.cloned.1.call-update) | async-done | bytes 131088 | tf_op jit(solution)/shard_map/reduce_scatter | solution.py:112
  586.3 1.5 convert_element_type.35
  (79 shorter events, 3.8 us)
Async XLA Ops:
  6.5 94.5 %copy-start = (bf16[2048,2,128]{2,1,0:T(2,128)(2,1)S(1)}, bf16[2048,2,128]{2,1,0:T(2,128)(2,1)}, u32[]{:S(2)}) copy-start(bf16[2048,2,128]{2,1,0:T(2,128)(2,1)} %param.16) | copy-start | bytes 3145732
  6.5 93.7 %all-reduce.2.cloned.1.call-start = ((), (), s32[]{:S(2)}) async-start(), calls=%async_computation.1 | async-start | bytes 2097152 | tf_op jit(solution)/shard_map/psum | solution.py:11
  7.3 96.2 %copy-start.1 = (bf16[2048,2,128]{2,1,0:T(2,128)(2,1)S(1)}, bf16[2048,2,128]{2,1,0:T(2,128)(2,1)}, u32[]{:S(2)}) copy-start(bf16[2048,2,128]{2,1,0:T(2,128)(2,1)} %param.17) | copy-start | bytes 3145732
  8.4 140.9 %all-gather.6.cloned.1.call-start = ((), (), s32[]{:S(2)}) async-start(), calls=%async_computation.2 | async-start | bytes 5242880 | tf_op jit(solution)/shard_map/all_gather | solution.py:98
  100.3 318.6 %all-gather.8.cloned.1.call-start = ((), (), s32[]{:S(2)}) async-start(), calls=%async_computation.4 | async-start | bytes 35651584 | tf_op jit(solution)/shard_map/all_gather | solution.py:15
  176.8 8.4 %copy-start.4 = (bf16[2048,1,128]{2,1,0:T(2,128)(2,1)S(1)}, bf16[2048,1,128]{2,1,0:T(2,128)(2,1)}, u32[]{:S(2)}) copy-start(bf16[2048,1,128]{2,1,0:T(2,128)(2,1)} %get-tuple-element.145) | copy-start | bytes 1572868
  185.3 10.3 %copy-start.3 = (bf16[2048,1,128]{2,1,0:T(2,128)(2,1)S(1)}, bf16[2048,1,128]{2,1,0:T(2,128)(2,1)}, u32[]{:S(2)}) copy-start(bf16[2048,1,128]{2,1,0:T(2,128)(2,1)} %get-tuple-element.144) | copy-start | bytes 1572868
  185.3 10.3 %copy-start.6 = (f32[512,4]{0,1:T(4,128)S(1)}, f32[512,4]{0,1:T(4,128)}, u32[]{:S(2)}) copy-start(f32[512,4]{0,1:T(4,128)} %get-tuple-element.151) | copy-start | bytes 24580
  195.6 4.7 copy-start.9
  195.6 4.7 copy-start.12
  200.3 1.6 copy-start.5
  200.4 1.6 copy-start.7
  200.4 1.5 copy-start.8
  205.8 380.6 %reduce-scatter.2.cloned.1.call-start = ((), (), s32[]{:S(2)}) async-start(), calls=%async_computation.3 | async-start | bytes 655360 | tf_op jit(solution)/shard_map/reduce_scatter | solution.py:112
  418.9 1.6 slice-start
Sparse Core Ops, SparseCore 0:
  10.6 89.6 all-reduce.1
  101.9 47.3 all-gather.5
  205.9 212.9 all-gather.7
  565.3 20.9 reduce-scatter.1
where the time goes:
time: 595 us; the launch traced here: 594 us
  waiting for transfers between devices  311 us (52%)
  other arithmetic  100 us (17%)
  local copies, waits for them, and re-layouts  63.1 us (11%)
  blocking collectives  58.7 us (10%)
  matrix products  46.1 us (8%)
  between operations  14.7 us (2%)
    all_gather x1, waiting for transfers between devices, joined(): pieces = jax.tree.map(lambda part: lax.all_gather(part, axis), value)  154 us
    psum x1, waiting for transfers between devices, spread(): return lax.psum(jnp.where(mine, shard, jnp.zeros_like(shard)), axis)  91.8 us
    add x16, other arithmetic, combine(): first[2] * first_scale[..., None] + second[2] * second_scale[..., None]  88.6 us
    all_gather x2, blocking collectives, joined(): pieces = jax.tree.map(lambda part: lax.all_gather(part, axis), value)  58.7 us
    all_gather x1, waiting for transfers between devices, local(): hidden_rows = lax.all_gather(hidden_rows, 'tp', axis=1, tiled=True)  43.4 us
    dynamic_slice x15, local copies, waits for them, and re-layouts, joined(): lax.scan(lambda running, section: (join(running, section), None), head, t...  26.2 us
    slice x3, local copies, waits for them, and re-layouts, joined(): tail = jax.tree.map(lambda part: part[1:], pieces)  21.6 us
    reduce_scatter x1, waiting for transfers between devices, local(): lax.psum_scatter(partial_out, 'tp', scatter_dimension=1, tiled=True)  21.1 us
  transfers between devices with their start and end apart: 4, of which 4 were waited for; matrix products, arithmetic and copies ran while one was open for 1% of the time, Pallas kernels for 0%

commit v1 on v0

v1 whole, which is shorter than its diff:
```python
import functools
import math

import jax
import jax.numpy as jnp
from jax import lax
from jax.experimental import pallas as pl
from jax.experimental.pallas import tpu as pltpu
from jax.sharding import PartitionSpec as P

CTX = 16
TP = 4
HEAD = 128
bf16 = jnp.bfloat16
f32 = jnp.float32


def dot(a, b):
    return jnp.dot(a, b, preferred_element_type=f32)


def dot_nt(a, b):
    return lax.dot_general(a, b, (((1,), (1,)), ((), ())), preferred_element_type=f32)


def project_kernel(t_ref, h0, h1, h2, h3, wq, wk, wv, out, acc):
    step = pl.program_id(0)
    for s, h in enumerate((h0, h1, h2, h3)):

        @pl.when(step == s)
        def _(h=h, s=s):
            rows = h[...]
            part = jnp.concatenate([dot(rows, wq[...]), dot(rows, wk[...]), dot(rows, wv[...])], 1)
            if s == 0:
                acc[...] = part
            elif s < TP - 1:
                acc[...] += part
            else:
                out[...] = (acc[...] + part).astype(bf16)


def project(t, pieces, w_query, w_key, w_value):
    rows, feats = pieces[0].shape
    width = w_query.shape[1] + w_key.shape[1] + w_value.shape[1]
    by_shift = lambda s, t: (lax.rem(t[0] + TP - s, TP), 0)
    fixed = lambda s, t: (0, 0)
    return pl.pallas_call(
        project_kernel,
        grid_spec=pltpu.PrefetchScalarGridSpec(
            num_scalar_prefetch=1,
            grid=(TP,),
            in_specs=[pl.BlockSpec((rows, feats), fixed)] * 4
            + [pl.BlockSpec((feats, w.shape[1]), by_shift) for w in (w_query, w_key, w_value)],
            out_specs=pl.BlockSpec((rows, width), fixed),
            scratch_shapes=[pltpu.VMEM((rows, width), f32)],
        ),
        out_shape=jax.ShapeDtypeStruct((rows, width), bf16),
        compiler_params=pltpu.CompilerParams(vmem_limit_bytes=24 * 2**20),
    )(t, *pieces, w_query, w_key, w_value)


def split3(x):
    hi = x.astype(bf16).astype(f32)
    mid = (x - hi).astype(bf16).astype(f32)
    return hi, mid, x - hi - mid


def attend_kernel(i_ref, q, kt, v, ks, vs, out, *, rows, chunk):
    step = pl.program_id(0)
    base = i_ref[0] * ks.shape[0]
    scale = (HEAD ** -0.5) * math.log2(math.e)
    groups = 4
    lane = lax.broadcasted_iota(jnp.int32, (rows, HEAD), 1)
    side = jnp.zeros((rows, HEAD), f32)
    keys = kt.shape[2]
    share = ks.shape[0]
    key_at = lax.broadcasted_iota(jnp.int32, (groups * rows, share), 1) + base
    row_at = lax.rem(lax.broadcasted_iota(jnp.int32, (groups * rows, share), 0), rows) + step * rows
    causal = key_at <= row_at
    ones = (lax.broadcasted_iota(jnp.int32, (share, HEAD), 1) == 0).astype(bf16)
    for kv in range(2):
        qh = jnp.concatenate(
            [q[:, (kv * groups + g) * HEAD : (kv * groups + g + 1) * HEAD] for g in range(groups)], 0
        )
        self_scores = dot_nt(qh, ks[:, kv * HEAD : (kv + 1) * HEAD])
        self_scores = jnp.where(causal, self_scores, -1e30)
        scores = [dot(qh, kt[kv, :, c : c + chunk]) for c in range(0, keys, chunk)]
        top = jnp.max(self_scores, -1, keepdims=True)
        for s in scores:
            top = jnp.maximum(top, jnp.max(s, -1, keepdims=True))
        weigh = lambda s: jnp.exp2((s - top) * scale).astype(bf16)
        acc = dot(weigh(self_scores), jnp.concatenate([vs[:, kv * HEAD : (kv + 1) * HEAD], ones], 1))
        for n, s in enumerate(scores):
            acc += dot(weigh(s), v[kv, n * chunk : (n + 1) * chunk, :])
        for g in range(groups):
            h = kv * groups + g
            part = acc[g * rows : (g + 1) * rows]
            out[:, h * HEAD : (h + 1) * HEAD] = part[:, :HEAD].astype(bf16)
            fields = split3(top[g * rows : (g + 1) * rows]) + split3(part[:, HEAD : HEAD + 1])
            for f, field in enumerate(fields):
                side = jnp.where(lane == f * 8 + h, field, side)
    out[:, 8 * HEAD : 9 * HEAD] = side.astype(bf16)


def attend(i, q, kt, v, ks, vs, rows=128, chunk=512):
    count, width = q.shape
    whole = lambda a: pl.BlockSpec(a.shape, lambda s, i: (0,) * a.ndim)
    return pl.pallas_call(
        functools.partial(attend_kernel, rows=rows, chunk=chunk),
        grid_spec=pltpu.PrefetchScalarGridSpec(
            num_scalar_prefetch=1,
            grid=(count // rows,),
            in_specs=[pl.BlockSpec((rows, width), lambda s, i: (s, 0))] + [whole(a) for a in (kt, v, ks, vs)],
            out_specs=pl.BlockSpec((rows, width + HEAD), lambda s, i: (s, 0)),
        ),
        out_shape=jax.ShapeDtypeStruct((count, width + HEAD), bf16),
        compiler_params=pltpu.CompilerParams(vmem_limit_bytes=40 * 2**20),
    )(i, q, kt, v, ks, vs)


def finish_kernel(t_ref, parts, w, out, att):
    scale = (HEAD ** -0.5) * math.log2(math.e)

    @pl.when(pl.program_id(0) == 0)
    def _():
        side = [parts[p, :, 8 * HEAD : 9 * HEAD].astype(f32) for p in range(CTX)]
        tops = [s[:, 0:8] + s[:, 8:16] + s[:, 16:24] for s in side]
        sums = [s[:, 24:32] + s[:, 32:40] + s[:, 40:48] for s in side]
        top = functools.reduce(jnp.maximum, tops)
        scales = [jnp.exp2((m - top) * scale) for m in tops]
        total = sum(a * b for a, b in zip(scales, sums))
        for h in range(8):
            acc = sum(
                parts[p, :, h * HEAD : (h + 1) * HEAD].astype(f32) * scales[p][:, h : h + 1] for p in range(CTX)
            )
            att[:, h * HEAD : (h + 1) * HEAD] = (acc / total[:, h : h + 1]).astype(bf16)

    out[0] = dot(att[...], w[...]).astype(bf16)


def finish(t, parts, w_out):
    _, share, width = parts.shape
    feats, cols = w_out.shape
    block = cols // TP
    return pl.pallas_call(
        finish_kernel,
        grid_spec=pltpu.PrefetchScalarGridSpec(
            num_scalar_prefetch=1,
            grid=(TP,),
            in_specs=[
                pl.BlockSpec(parts.shape, lambda s, t: (0, 0, 0)),
                pl.BlockSpec((feats, block), lambda s, t: (0, lax.rem(t[0] + s, TP))),
            ],
            out_specs=pl.BlockSpec((1, share, block), lambda s, t: (s, 0, 0)),
            scratch_shapes=[pltpu.VMEM((share, feats), bf16)],
        ),
        out_shape=jax.ShapeDtypeStruct((TP, share, block), bf16),
        compiler_params=pltpu.CompilerParams(vmem_limit_bytes=24 * 2**20),
    )(t, parts, w_out)


def shift(x, s):
    return lax.ppermute(x, "tp", [(i, (i + s) % TP) for i in range(TP)])


def local(response, owner, doc_lengths, doc_keys, doc_values, w_query, w_key, w_value, w_out):
    i = lax.axis_index("ctx").astype(jnp.int32).reshape(1)
    t = lax.axis_index("tp").astype(jnp.int32).reshape(1)
    count, feats = response.shape[1:]
    share = count // CTX
    cache = doc_keys.shape[0]
    visible = (jnp.arange(cache) < doc_lengths[0])[:, None, None]
    keys_t = jnp.where(visible, doc_keys, doc_keys[:1]).transpose(1, 2, 0)
    side = jnp.broadcast_to((jnp.arange(HEAD) == 0)[None, None, :], doc_values.shape).astype(bf16)
    values = jnp.where(visible, jnp.concatenate([doc_values, side], 2), 0).transpose(1, 0, 2)

    chunks = lax.all_to_all(response[0].reshape(CTX, share, feats), "ctx", 0, 0)
    mine = lax.dynamic_index_in_dim(chunks, owner[0], 0, keepdims=False)
    pieces = [mine] + [shift(mine, s) for s in range(1, TP)]
    qkv = project(t, pieces, w_query, w_key, w_value)
    width = w_query.shape[1]
    kv_width = w_key.shape[1]
    queries = lax.all_to_all(jnp.broadcast_to(qkv[None, :, :width], (CTX, share, width)), "ctx", 0, 0)
    sent = attend(
        i,
        queries.reshape(count, width),
        keys_t,
        values,
        qkv[:, width : width + kv_width],
        qkv[:, width + kv_width :],
    )
    parts = lax.all_to_all(sent.reshape(CTX, share, width + HEAD), "ctx", 0, 0)
    partial_out = finish(t, parts, w_out)
    out = partial_out[0].astype(f32)
    for s in range(1, TP):
        out += shift(partial_out[s], s).astype(f32)
    return out.astype(bf16)


def solution(mesh):
    placed = (
        P(("dp", "ctx"), None, "tp"),
        P("dp"),
        P(("dp", "ctx")),
        P(("dp", "ctx"), "tp", None),
        P(("dp", "ctx"), "tp", None),
        P(None, "tp"),
        P(None, "tp"),
        P(None, "tp"),
        P("tp", None),
    )
    return jax.shard_map(
        local, mesh=mesh, in_specs=placed, out_specs=P(("dp", "ctx"), "tp"), check_vma=False
    )
```

time: 595 us -> 109 us (0.18)
  waiting for transfers between devices: 311 us -> 30.1 us
  other arithmetic: 100 us -> 4.55 us
  matrix products: 46.1 us -> 0 us
  local copies, waits for them, and re-layouts: 63.1 us -> 17.5 us
  blocking collectives: 58.7 us -> 17.4 us
  starting transfers between devices: 0.12 us -> 19.7 us
  Pallas kernels: 0 us -> 18 us
  between operations: 14.7 us -> 1.38 us
    all_gather x2 -> x0, waiting for transfers between devices: 198 us -> none  [the longest x1 154 us: joined(): pieces = jax.tree.map(lambda part: lax.all_gather(part, axis), value)]
    psum x1 -> x0, waiting for transfers between devices: 91.8 us -> none  [spread(): return lax.psum(jnp.where(mine, shard, jnp.zeros_like(shard)), axis)]
    add x32 -> x0, other arithmetic: 89 us -> none  [the longest x16 88.6 us: combine(): first[2] * first_scale[..., None] + second[2] * second_scale[..., None]]
    all_gather x2 -> x0, blocking collectives: 58.7 us -> none  [joined(): pieces = jax.tree.map(lambda part: lax.all_gather(part, axis), value)]
    dot_general x6 -> x0, matrix products: 46.1 us -> none  [the longest x2 16.4 us: attend(): jnp.einsum('rgd,kd->rgk', query_heads[:, kv_head], key_block[:, kv_head],...]
    slice x10 -> x2, local copies, waits for them, and re-layouts: 29.3 us -> 0.02 us  [the longest x1 0.01 us: local(): qkv[None, :, :width]]
    dynamic_slice x17 -> x0, local copies, waits for them, and re-layouts: 26.4 us -> none  [the longest x15 26.2 us: joined(): lax.scan(lambda running, section: (join(running, section), None), head, t...]
    reduce_scatter x1 -> x0, waiting for transfers between devices: 21.1 us -> none  [local(): lax.psum_scatter(partial_out, 'tp', scatter_dimension=1, tiled=True)]
  transfers between devices with their start and end apart: 4 -> 8, of which waited for: 4 -> 8; matrix products, arithmetic and copies ran while one was open for 1% -> 10% of each run, Pallas kernels for 0% -> 0%
where the time goes in v1:
time: 109 us
  waiting for transfers between devices  30.1 us (28%)
  starting transfers between devices  19.7 us (18%)
  Pallas kernels  18 us (17%)
  local copies, waits for them, and re-layouts  17.5 us (16%)
  blocking collectives  17.4 us (16%)
  other arithmetic  4.55 us (4%)
  between operations  1.38 us (1%)
    all_to_all x1, blocking collectives, local(): parts = lax.all_to_all(sent.reshape(CTX, share, width + HEAD), 'ctx', 0, 0)  17.4 us
    unnamed x12, local copies, waits for them, and re-layouts  15.7 us
    all_to_all x1, waiting for transfers between devices, local(): chunks = lax.all_to_all(response[0].reshape(CTX, share, feats), 'ctx', 0, 0)  14 us
    pallas_call x1, Pallas kernels, attend(): pl.pallas_call(functools.partial(attend_kernel, rows=rows, chunk=chunk),...  12.2 us
    ppermute x6, waiting for transfers between devices, shift(): return lax.ppermute(x, 'tp', [(i, (i + s) % TP) for i in range(TP)])  10.5 us
    all_to_all x1, starting transfers between devices, local(): chunks = lax.all_to_all(response[0].reshape(CTX, share, feats), 'ctx', 0, 0)  8.26 us
    ppermute x6, starting transfers between devices, shift(): return lax.ppermute(x, 'tp', [(i, (i + s) % TP) for i in range(TP)])  7.74 us
    all_to_all x1, waiting for transfers between devices, local(): lax.all_to_all(jnp.broadcast_to(qkv[None, :, :width], (CTX, share, width)...  5.54 us
  transfers between devices with their start and end apart: 8, of which 8 were waited for; matrix products, arithmetic and copies ran while one was open for 10% of the time, Pallas kernels for 0%

profile of v1, /device:TPU:0, one launch (start us, length us, event | category | flops | bytes accessed | tf_op | source)
XLA Modules:
  0.0 108.6 jit_solution(5051337180295696340)
XLA Ops:
  0.0 0.0 copy-start.3
  0.0 8.3 %all-to-all-start = ((bf16[16,32,1024]{2,1,0:T(8,128)(2,1)}), bf16[16,32,1024]{2,1,0:T(8,128)(2,1)S(1)}, u32[]{:S(2)}, u32[]{:S(2)}) async-start(bf16[16,32,1024]{2,1,0:T(8,128)(2,1)} %bitcast.32), calls=%async_computation | async-start | bytes 2097152 | tf_op jit(solution)/shard_map/all_to_all | solution.py:177
  9.6 2.4 %copy.11 = bf16[2048,2,128]{2,0,1:T(8,128)(2,1)} copy(bf16[2048,2,128]{2,1,0:T(2,128)(2,1)} %param.13) | data formatting | bytes 2097152 | tf_op args[4]
  11.9 14.0 %all-to-all-done = bf16[16,32,1024]{2,1,0:T(8,128)(2,1)S(1)} async-done(((bf16[16,32,1024]{2,1,0:T(8,128)(2,1)}), bf16[16,32,1024]{2,1,0:T(8,128)(2,1)S(1)}, u32[]{:S(2)}, u32[]{:S(2)}) %all-to-all-start) | async-done | bytes 1048608 | tf_op jit(solution)/shard_map/all_to_all | solution.py:177
  26.0 2.8 %collective-permute-start.2 = (bf16[32,1024]{1,0:T(8,128)(2,1)S(1)}, bf16[32,1024]{1,0:T(8,128)(2,1)S(1)}, u32[]{:S(2)}, u32[]{:S(2)}) collective-permute-start(bf16[32,1024]{1,0:T(8,128)(2,1)S(1)} %dynamic-slice_bitcast_fusion.h0), channel_id=1, source_target_pairs={{0,3},{1,0},{2,1},{3,2},{4,7},{5,4},{6,5},{7,6},{8,11},{9,8},{10,9... | collective-permute-start | bytes 196616 | tf_op jit(solution)/shard_map/ppermute | solution.py:163
  28.7 0.8 collective-permute-start.1
  29.5 0.9 collective-permute-start
  30.4 0.2 collective-permute-done.2.h3
  30.6 3.9 %collective-permute-done.1.h2 = bf16[32,1024]{1,0:T(8,128)(2,1)S(1)} collective-permute-done((bf16[32,1024]{1,0:T(8,128)(2,1)S(1)}, bf16[32,1024]{1,0:T(8,128)(2,1)S(1)}, u32[]{:S(2)}, u32[]{:S(2)}) %collective-permute-start.1) | collective-permute-done | bytes 65568 | tf_op jit(solution)/shard_map/ppermute | solution.py:163
  34.5 0.7 collective-permute-done.h1
  35.2 0.0 copy-done.3
  35.2 0.0 copy-start
  35.2 3.4 %copy-done = bf16[4096,1024]{1,0:T(8,128)(2,1)S(1)} copy-done((bf16[4096,1024]{1,0:T(8,128)(2,1)S(1)}, bf16[4096,1024]{1,0:T(8,128)(2,1)}, u32[]{:S(2)}) %copy-start) | copy-done | bytes 8388632
  38.6 0.0 copy-start.4
  38.6 1.6 %copy-done.4 = bf16[4096,256]{1,0:T(8,128)(2,1)S(1)} copy-done((bf16[4096,256]{1,0:T(8,128)(2,1)S(1)}, bf16[4096,256]{1,0:T(8,128)(2,1)}, u32[]{:S(2)}) %copy-start.4) | copy-done | bytes 2097176
  40.2 2.6 %shard_map.91 = bf16[32,1536]{1,0:T(8,128)(2,1)S(1)} custom-call(s32[1]{0:T(128)} %bitcast.t_ref, bf16[32,1024]{1,0:T(8,128)(2,1)S(1)} %dynamic-slice_bitcast_fusion.h0, bf16[32,1024]{1,0:T(8,128)(2,1)S(1)} %collective-permute-done.h1, bf16[32,1024]{1,0:T(8,128)(2,1)S(1)} %collective-permute-done.1.h2, bf16[32,1024]{1,0:T(8,128)(2,1)S(1)} %collective-permute-done.2.h3, ...), custom_call_target="tpu_custom_call" | custom-call | tf_op jit(solution)/shard_map/pallas_call | solution.py:47
  42.8 1.1 %broadcast_in_dim.43 = bf16[16,32,1024]{2,1,0:T(8,128)(2,1)} broadcast(bf16[32,1024]{1,0:T(8,128)(2,1)S(1)} %slice.32), dimensions={1,2} | broadcast | bytes 1114112 | tf_op jit(solution)/shard_map/broadcast_in_dim | solution.py:183
  43.9 3.7 %all-to-all-start.1 = ((bf16[16,32,1024]{2,1,0:T(8,128)(2,1)}), bf16[16,32,1024]{2,1,0:T(8,128)(2,1)S(1)}, u32[]{:S(2)}, u32[]{:S(2)}) async-start(bf16[16,32,1024]{2,1,0:T(8,128)(2,1)} %broadcast_in_dim.43), calls=%async_computation.1 | async-start | bytes 2097152 | tf_op jit(solution)/shard_map/all_to_all | solution.py:183
  47.6 1.5 %fusion.v = bf16[2,2048,256]{2,1,0:T(8,128)(2,1)S(1)} fusion(bf16[2048,2,128]{2,0,1:T(8,128)(2,1)} %copy.11, pred[2048]{0:T(1024)(128)(4,1)S(1)} %iota_compare_fusion, bf16[256]{0:T(256)(128)(2,1)S(1)} %pad.1.clone), kind=kLoop, calls=%fused_computation.1 | loop fusion | flops 5242880 | bytes 3148288 | tf_op jit(solution)/shard_map/transpose | solution.py:175
  49.1 3.7 %copy.10 = bf16[2048,2,128]{0,2,1:T(8,128)(2,1)} copy(bf16[2048,2,128]{2,1,0:T(2,128)(2,1)} %param.12) | data formatting | bytes 2097152 | tf_op args[3]
  52.8 0.7 slice_bitcast_fusion.4
  53.5 2.3 %select_bitcast_fusion.kt = bf16[2,128,2048]{2,1,0:T(8,128)(2,1)} fusion(bf16[2048,2,128]{0,2,1:T(8,128)(2,1)} %copy.10, pred[2048]{0:T(1024)(128)(4,1)S(1)} %iota_compare_fusion, bf16[2,128]{1,0:T(2,128)(2,1)S(1)} %slice_bitcast_fusion.4), kind=kLoop, calls=%fused_computation.2 | loop fusion | flops 524288 | bytes 2099712 | tf_op jit(solution)/shard_map/transpose | solution.py:173
  55.8 5.5 %all-to-all-done.1 = bf16[16,32,1024]{2,1,0:T(8,128)(2,1)S(1)} async-done(((bf16[16,32,1024]{2,1,0:T(8,128)(2,1)}), bf16[16,32,1024]{2,1,0:T(8,128)(2,1)S(1)}, u32[]{:S(2)}, u32[]{:S(2)}) %all-to-all-start.1) | async-done | bytes 1048608 | tf_op jit(solution)/shard_map/all_to_all | solution.py:183
  61.4 0.0 copy-start.2
  61.4 1.2 %copy-done.2 = bf16[2,128,2048]{2,1,0:T(8,128)(2,1)S(1)} copy-done((bf16[2,128,2048]{2,1,0:T(8,128)(2,1)S(1)}, bf16[2,128,2048]{2,1,0:T(8,128)(2,1)}, u32[]{:S(2)}) %copy-start.2) | copy-done | bytes 1048600
  62.6 12.2 %shard_map.92 = bf16[512,1152]{1,0:T(8,128)(2,1)S(1)} custom-call(s32[1]{0:T(128)} %bitcast.1.i_ref, bf16[512,1024]{1,0:T(8,128)(2,1)S(1)} %bitcast.31, bf16[2,128,2048]{2,1,0:T(8,128)(2,1)S(1)} %copy-done.2, bf16[2,2048,256]{2,1,0:T(8,128)(2,1)S(1)} %fusion.v, bf16[32,256]{1,0:T(8,128)(2,1)S(1)} %get-tuple-element.9.ks, bf16[32,256]{1,0:T(8,128)(2,1)S(1)} %get-tuple-element.8.vs), custom_call_target="tpu_custom_call" | custom-call | tf_op jit(solution)/shard_map/pallas_call | solution.py:108
  74.8 17.4 %all_to_all.15.parts = bf16[16,32,1152]{2,1,0:T(8,128)(2,1)S(1)} all-to-all(bf16[16,32,1152]{2,1,0:T(8,128)(2,1)S(1)} %bitcast.30), channel_id=1, replica_groups=mesh['dp'=2,'ctx'=16,'tp'=4] {'ctx'}, dimensions={0} | all-to-all | bytes 2359296 | tf_op jit(solution)/shard_map/all_to_all | solution.py:192
  92.2 0.0 copy-start.1
  92.2 3.4 %copy-done.1 = bf16[1024,4096]{1,0:T(8,128)(2,1)S(1)} copy-done((bf16[1024,4096]{1,0:T(8,128)(2,1)S(1)}, bf16[1024,4096]{1,0:T(8,128)(2,1)}, u32[]{:S(2)}) %copy-start.1) | copy-done | bytes 8388632
  95.5 3.3 %shard_map.93 = bf16[4,32,1024]{2,1,0:T(8,128)(2,1)S(1)} custom-call(s32[1]{0:T(128)} %bitcast.t_ref, bf16[16,32,1152]{2,1,0:T(8,128)(2,1)S(1)} %all_to_all.15.parts, bf16[1024,4096]{1,0:T(8,128)(2,1)S(1)} %copy-done.1), custom_call_target="tpu_custom_call" | custom-call | tf_op jit(solution)/shard_map/pallas_call | solution.py:145
  98.9 0.1 collective-permute-start.3
  98.9 3.2 %collective-permute-start.5 = (bf16[32,1024]{1,0:T(8,128)(2,1)S(1)}, bf16[32,1024]{1,0:T(8,128)(2,1)S(1)}, u32[]{:S(2)}, u32[]{:S(2)}) collective-permute-start(bf16[32,1024]{1,0:T(8,128)(2,1)S(1)} %get-tuple-element.6), channel_id=1, source_target_pairs={{0,3},{1,0},{2,1},{3,2},{4,7},{5,4},{6,5},{7,6},{8,11},{9,8},{10,9... | collective-permute-start | bytes 196616 | tf_op jit(solution)/shard_map/ppermute | solution.py:163
  102.2 0.0 collective-permute-start.4
  102.2 2.2 %collective-permute-done.3 = bf16[32,1024]{1,0:T(8,128)(2,1)S(1)} collective-permute-done((bf16[32,1024]{1,0:T(8,128)(2,1)S(1)}, bf16[32,1024]{1,0:T(8,128)(2,1)S(1)}, u32[]{:S(2)}, u32[]{:S(2)}) %collective-permute-start.3) | collective-permute-done | bytes 65568 | tf_op jit(solution)/shard_map/ppermute | solution.py:163
  104.4 0.3 collective-permute-done.5
  104.7 3.3 %collective-permute-done.4 = bf16[32,1024]{1,0:T(8,128)(2,1)S(1)} collective-permute-done((bf16[32,1024]{1,0:T(8,128)(2,1)S(1)}, bf16[32,1024]{1,0:T(8,128)(2,1)S(1)}, u32[]{:S(2)}, u32[]{:S(2)}) %collective-permute-start.4) | collective-permute-done | bytes 65568 | tf_op jit(solution)/shard_map/ppermute | solution.py:163
  107.9 0.7 fusion.3
  (7 shorter events, 0.1 us)
Async XLA Ops:
  0.0 35.2 %copy-start.3 = (bf16[4096,256]{1,0:T(8,128)(2,1)S(1)}, bf16[4096,256]{1,0:T(8,128)(2,1)}, u32[]{:S(2)}) copy-start(bf16[4096,256]{1,0:T(8,128)(2,1)} %wk.1) | copy-start | bytes 6291460
  0.0 26.0 %all-to-all-start = ((bf16[16,32,1024]{2,1,0:T(8,128)(2,1)}), bf16[16,32,1024]{2,1,0:T(8,128)(2,1)S(1)}, u32[]{:S(2)}, u32[]{:S(2)}) async-start(bf16[16,32,1024]{2,1,0:T(8,128)(2,1)} %bitcast.32), calls=%async_computation | async-start | bytes 2097152 | tf_op jit(solution)/shard_map/all_to_all | solution.py:177
  26.0 4.7 %collective-permute-start.2 = (bf16[32,1024]{1,0:T(8,128)(2,1)S(1)}, bf16[32,1024]{1,0:T(8,128)(2,1)S(1)}, u32[]{:S(2)}, u32[]{:S(2)}) collective-permute-start(bf16[32,1024]{1,0:T(8,128)(2,1)S(1)} %dynamic-slice_bitcast_fusion.h0), channel_id=1, source_target_pairs={{0,3},{1,0},{2,1},{3,2},{4,7},{5,4},{6,5},{7,6},{8,11},{9,8},{10,9... | collective-permute-start | bytes 196616 | tf_op jit(solution)/shard_map/ppermute | solution.py:163
  28.7 5.8 %collective-permute-start.1 = (bf16[32,1024]{1,0:T(8,128)(2,1)S(1)}, bf16[32,1024]{1,0:T(8,128)(2,1)S(1)}, u32[]{:S(2)}, u32[]{:S(2)}) collective-permute-start(bf16[32,1024]{1,0:T(8,128)(2,1)S(1)} %dynamic-slice_bitcast_fusion.h0), channel_id=1, source_target_pairs={{0,2},{1,3},{2,0},{3,1},{4,6},{5,7},{6,4},{7,5},{8,10},{9,11},{10,... | collective-permute-start | bytes 196616 | tf_op jit(solution)/shard_map/ppermute | solution.py:163
  29.5 5.7 %collective-permute-start = (bf16[32,1024]{1,0:T(8,128)(2,1)S(1)}, bf16[32,1024]{1,0:T(8,128)(2,1)S(1)}, u32[]{:S(2)}, u32[]{:S(2)}) collective-permute-start(bf16[32,1024]{1,0:T(8,128)(2,1)S(1)} %dynamic-slice_bitcast_fusion.h0), channel_id=1, source_target_pairs={{0,1},{1,2},{2,3},{3,0},{4,5},{5,6},{6,7},{7,4},{8,9},{9,10},{10,1... | collective-permute-start | bytes 196616 | tf_op jit(solution)/shard_map/ppermute | solution.py:163
  35.2 3.4 %copy-start = (bf16[4096,1024]{1,0:T(8,128)(2,1)S(1)}, bf16[4096,1024]{1,0:T(8,128)(2,1)}, u32[]{:S(2)}) copy-start(bf16[4096,1024]{1,0:T(8,128)(2,1)} %wq.1) | copy-start | bytes 25165828
  38.6 1.6 %copy-start.4 = (bf16[4096,256]{1,0:T(8,128)(2,1)S(1)}, bf16[4096,256]{1,0:T(8,128)(2,1)}, u32[]{:S(2)}) copy-start(bf16[4096,256]{1,0:T(8,128)(2,1)} %wv.1) | copy-start | bytes 6291460
  43.9 17.5 %all-to-all-start.1 = ((bf16[16,32,1024]{2,1,0:T(8,128)(2,1)}), bf16[16,32,1024]{2,1,0:T(8,128)(2,1)S(1)}, u32[]{:S(2)}, u32[]{:S(2)}) async-start(bf16[16,32,1024]{2,1,0:T(8,128)(2,1)} %broadcast_in_dim.43), calls=%async_computation.1 | async-start | bytes 2097152 | tf_op jit(solution)/shard_map/all_to_all | solution.py:183
  61.4 1.2 %copy-start.2 = (bf16[2,128,2048]{2,1,0:T(8,128)(2,1)S(1)}, bf16[2,128,2048]{2,1,0:T(8,128)(2,1)}, u32[]{:S(2)}) copy-start(bf16[2,128,2048]{2,1,0:T(8,128)(2,1)} %select_bitcast_fusion.kt) | copy-start | bytes 3145732
  92.2 3.4 %copy-start.1 = (bf16[1024,4096]{1,0:T(8,128)(2,1)S(1)}, bf16[1024,4096]{1,0:T(8,128)(2,1)}, u32[]{:S(2)}) copy-start(bf16[1024,4096]{1,0:T(8,128)(2,1)} %w.1) | copy-start | bytes 25165828
  98.9 5.5 %collective-permute-start.3 = (bf16[32,1024]{1,0:T(8,128)(2,1)S(1)}, bf16[32,1024]{1,0:T(8,128)(2,1)S(1)}, u32[]{:S(2)}, u32[]{:S(2)}) collective-permute-start(bf16[32,1024]{1,0:T(8,128)(2,1)S(1)} %get-tuple-element.5), channel_id=1, source_target_pairs={{0,1},{1,2},{2,3},{3,0},{4,5},{5,6},{6,7},{7,4},{8,9},{9,10},{10,1... | collective-permute-start | bytes 196616 | tf_op jit(solution)/shard_map/ppermute | solution.py:163
  98.9 5.7 %collective-permute-start.5 = (bf16[32,1024]{1,0:T(8,128)(2,1)S(1)}, bf16[32,1024]{1,0:T(8,128)(2,1)S(1)}, u32[]{:S(2)}, u32[]{:S(2)}) collective-permute-start(bf16[32,1024]{1,0:T(8,128)(2,1)S(1)} %get-tuple-element.6), channel_id=1, source_target_pairs={{0,3},{1,0},{2,1},{3,2},{4,7},{5,4},{6,5},{7,6},{8,11},{9,8},{10,9... | collective-permute-start | bytes 196616 | tf_op jit(solution)/shard_map/ppermute | solution.py:163
  102.2 5.8 %collective-permute-start.4 = (bf16[32,1024]{1,0:T(8,128)(2,1)S(1)}, bf16[32,1024]{1,0:T(8,128)(2,1)S(1)}, u32[]{:S(2)}, u32[]{:S(2)}) collective-permute-start(bf16[32,1024]{1,0:T(8,128)(2,1)S(1)} %get-tuple-element.7), channel_id=1, source_target_pairs={{0,2},{1,3},{2,0},{3,1},{4,6},{5,7},{6,4},{7,5},{8,10},{9,11},{10,... | collective-permute-start | bytes 196616 | tf_op jit(solution)/shard_map/ppermute | solution.py:163

commit v2 on v1

v2 whole, which is shorter than its diff:
```python
import functools
import math

import jax
import jax.numpy as jnp
from jax import lax
from jax.experimental import pallas as pl
from jax.experimental.pallas import tpu as pltpu
from jax.sharding import PartitionSpec as P

CTX = 16
TP = 4
HEAD = 128
bf16 = jnp.bfloat16
f32 = jnp.float32


def dot(a, b):
    return jnp.dot(a, b, preferred_element_type=f32)


def dot_nt(a, b):
    return lax.dot_general(a, b, (((1,), (1,)), ((), ())), preferred_element_type=f32)


def begin_kernel(h, wk, wv, keys, values):
    feats = h.shape[1]
    start = pl.multiple_of(lax.axis_index("tp") * feats, feats)
    for w, out in ((wk, keys), (wv, values)):
        out[...] = dot(h[...], w[pl.ds(start, feats), :])


def begin(mine, w_key, w_value):
    vmem = pl.BlockSpec(memory_space=pltpu.VMEM)
    return pl.pallas_call(
        begin_kernel,
        in_specs=[vmem] * 3,
        out_specs=[vmem] * 2,
        out_shape=[jax.ShapeDtypeStruct((mine.shape[0], w.shape[1]), f32) for w in (w_key, w_value)],
        compiler_params=pltpu.CompilerParams(vmem_limit_bytes=6 * 2**20),
        cost_estimate=pl.CostEstimate(flops=0, bytes_accessed=48 * 2**20, transcendentals=0),
    )(mine, w_key, w_value)


def project_kernel(h0, h1, h2, h3, k0, v0, wq, wk, wv, queries, keys, values):
    feats = h0.shape[1]
    totals = [0.0, k0[...], v0[...]]
    for s, h in enumerate((h0, h1, h2, h3)):
        start = pl.multiple_of(lax.rem(lax.axis_index("tp") + TP - s, TP) * feats, feats)
        rows = h[...]
        for m, w in enumerate((wq, wk, wv)):
            if s > 0 or m == 0:
                totals[m] = totals[m] + dot(rows, w[pl.ds(start, feats), :])
    q = totals[0].astype(bf16)
    for c in range(CTX):
        queries[c] = q
    keys[...] = totals[1].astype(bf16)
    values[...] = totals[2].astype(bf16)


def project(pieces, begun, w_query, w_key, w_value):
    rows, feats = pieces[0].shape
    vmem = pl.BlockSpec(memory_space=pltpu.VMEM)
    shapes = [(CTX, rows, w_query.shape[1]), (rows, w_key.shape[1]), (rows, w_value.shape[1])]
    return pl.pallas_call(
        project_kernel,
        in_specs=[vmem] * 9,
        out_specs=[vmem] * 3,
        out_shape=[jax.ShapeDtypeStruct(s, bf16) for s in shapes],
        compiler_params=pltpu.CompilerParams(vmem_limit_bytes=6 * 2**20),
    )(*pieces, *begun, w_query, w_key, w_value)


def split3(x):
    hi = x.astype(bf16).astype(f32)
    mid = (x - hi).astype(bf16).astype(f32)
    return hi, mid, x - hi - mid


def attend_kernel(len_ref, q, k, v, ks, vs, out, *, rows, chunk):
    scale = (HEAD ** -0.5) * math.log2(math.e)
    groups = 4
    keys = k.shape[1]
    share = ks.shape[0]
    starts = range(0, keys, chunk)
    units = [(r, kv) for r in range(0, q.shape[0], rows) for kv in range(2)]
    lane = lax.broadcasted_iota(jnp.int32, (rows, HEAD), 1)
    key_at = lax.broadcasted_iota(jnp.int32, (groups * rows, share), 1) + lax.axis_index("ctx") * share
    row_at = lax.rem(lax.broadcasted_iota(jnp.int32, (groups * rows, share), 0), rows)
    ones = (lax.broadcasted_iota(jnp.int32, (share, HEAD), 1) == 0).astype(bf16)
    chunk_at = lax.broadcasted_iota(jnp.int32, (chunk, HEAD), 0)
    chunk_lane = lax.broadcasted_iota(jnp.int32, (chunk, HEAD), 1)
    counted = [
        jnp.where((chunk_at < len_ref[0] - c) & (chunk_lane == 0), 1.0, 0.0).astype(bf16) for c in starts
    ]

    def heads_of(r, kv):
        cols = [(kv * groups + g) * HEAD for g in range(groups)]
        return jnp.concatenate([q[r : r + rows, c : c + HEAD] for c in cols], 0)

    def of_kv(ref, kv):
        return ref[:, kv * HEAD : (kv + 1) * HEAD]

    heads = heads_of(*units[0])
    scores = [dot_nt(heads, k[0, c : c + chunk, :]) for c in starts]
    for n, (r, kv) in enumerate(units):
        self_scores = jnp.where(key_at <= row_at + r, dot_nt(heads, of_kv(ks, kv)), -1e30)
        tops = [s[:, c : c + HEAD] for s in scores for c in range(0, chunk, HEAD)]
        top = jnp.max(functools.reduce(jnp.maximum, tops), -1, keepdims=True)
        top = jnp.maximum(top, jnp.max(self_scores, -1, keepdims=True))
        weigh = lambda s: jnp.exp2((s - top) * scale).astype(bf16)
        acc = dot(weigh(self_scores), jnp.concatenate([of_kv(vs, kv), ones], 1))
        after = units[n + 1] if n + 1 < len(units) else None
        if after:
            heads = heads_of(*after)
        upcoming = []
        for c, s, count in zip(starts, scores, counted):
            if after:
                upcoming.append(dot_nt(heads, k[after[1], c : c + chunk, :]))
            acc += dot(weigh(s), jnp.concatenate([v[kv, c : c + chunk, :], count], 1))
        scores = upcoming
        if kv == 0:
            tops_at = sums_at = jnp.zeros((rows, HEAD), f32)
        for g in range(groups):
            h = kv * groups + g
            part = acc[g * rows : (g + 1) * rows]
            out[r : r + rows, h * HEAD : (h + 1) * HEAD] = part[:, :HEAD].astype(bf16)
            tops_at = jnp.where(lane == h, top[g * rows : (g + 1) * rows], tops_at)
            sums_at = jnp.where(lane == h, part[:, HEAD : HEAD + 1], sums_at)
        if kv == 1:
            fields = split3(tops_at) + split3(sums_at)
            side = fields[0] + sum(pltpu.roll(x, 8 * f, 1) for f, x in enumerate(fields) if f)
            out[r : r + rows, 8 * HEAD : 9 * HEAD] = side.astype(bf16)


def attend(length, q, k, v, ks, vs, rows=128, chunk=512):
    count, width = q.shape
    vmem = pl.BlockSpec(memory_space=pltpu.VMEM)
    smem = pl.BlockSpec(memory_space=pltpu.SMEM)
    return pl.pallas_call(
        functools.partial(attend_kernel, rows=rows, chunk=chunk),
        in_specs=[smem] + [vmem] * 5,
        out_specs=vmem,
        out_shape=jax.ShapeDtypeStruct((count, width + HEAD), bf16),
        compiler_params=pltpu.CompilerParams(vmem_limit_bytes=24 * 2**20),
        cost_estimate=pl.CostEstimate(flops=0, bytes_accessed=32 * 2**20, transcendentals=0),
    )(length, q, k, v, ks, vs)


def finish_kernel(parts, w, out):
    scale = (HEAD ** -0.5) * math.log2(math.e)
    block = out.shape[2]
    starts = [pl.multiple_of(lax.rem(lax.axis_index("tp") + s, TP) * block, block) for s in range(TP)]
    side = [parts[p, :, 8 * HEAD : 9 * HEAD].astype(f32) for p in range(CTX)]
    tops = [s[:, 0:8] + s[:, 8:16] + s[:, 16:24] for s in side]
    sums = [s[:, 24:32] + s[:, 32:40] + s[:, 40:48] for s in side]
    top = functools.reduce(jnp.maximum, tops)
    scales = [jnp.exp2((m - top) * scale) for m in tops]
    total = sum(a * b for a, b in zip(scales, sums))
    heads = []
    for h in range(8):
        acc = sum(parts[p, :, h * HEAD : (h + 1) * HEAD].astype(f32) * scales[p][:, h : h + 1] for p in range(CTX))
        heads.append((acc / total[:, h : h + 1]).astype(bf16))
    attended = jnp.concatenate(heads, 1)
    for s in range(TP):
        out[s] = dot(attended, w[:, pl.ds(starts[s], block)]).astype(bf16)


def finish(parts, w_out):
    _, share, width = parts.shape
    feats, cols = w_out.shape
    block = cols // TP
    vmem = pl.BlockSpec(memory_space=pltpu.VMEM)
    return pl.pallas_call(
        finish_kernel,
        in_specs=[vmem, vmem],
        out_specs=vmem,
        out_shape=jax.ShapeDtypeStruct((TP, share, block), bf16),
        compiler_params=pltpu.CompilerParams(vmem_limit_bytes=6 * 2**20),
        cost_estimate=pl.CostEstimate(
            flops=2 * share * feats * cols, bytes_accessed=2 * w_out.size, transcendentals=0
        ),
    )(parts, w_out)


def shift(x, s):
    return lax.ppermute(x, "tp", [(i, (i + s) % TP) for i in range(TP)])


def local(response, owner, doc_lengths, doc_keys, doc_values, w_query, w_key, w_value, w_out):
    count, feats = response.shape[1:]
    share = count // CTX
    cache = doc_keys.shape[0]
    chunks = lax.all_to_all(response[0].reshape(CTX, share, feats), "ctx", 0, 0)
    chunks, owner, doc_lengths, doc_keys, doc_values = lax.optimization_barrier(
        (chunks, owner, doc_lengths, doc_keys, doc_values)
    )
    mine = lax.dynamic_index_in_dim(chunks, owner[0], 0, keepdims=False)
    pieces = [mine] + [shift(mine, s) for s in range(1, TP)]
    visible = (jnp.arange(cache) < doc_lengths[0])[:, None, None]
    keys = jnp.where(visible, doc_keys, doc_keys[:1]).transpose(1, 0, 2)
    values = jnp.where(visible, doc_values, 0).transpose(1, 0, 2)
    begun = begin(mine, w_key, w_value)
    queries, self_keys, self_values = project(pieces, begun, w_query, w_key, w_value)
    queries, keys, values, self_keys, self_values, doc_lengths = lax.optimization_barrier(
        (queries, keys, values, self_keys, self_values, doc_lengths)
    )
    queries = lax.all_to_all(queries, "ctx", 0, 0).reshape(count, -1)
    sent = attend(doc_lengths, queries, keys, values, self_keys, self_values)
    parts = lax.all_to_all(sent.reshape(CTX, share, -1), "ctx", 0, 0)
    partial_out = finish(parts, w_out)
    out = partial_out[0].astype(f32)
    for s in range(1, TP):
        out += shift(partial_out[s], s).astype(f32)
    return out.astype(bf16)


def solution(mesh):
    placed = (
        P(("dp", "ctx"), None, "tp"),
        P("dp"),
        P(("dp", "ctx")),
        P(("dp", "ctx"), "tp", None),
        P(("dp", "ctx"), "tp", None),
        P(None, "tp"),
        P(None, "tp"),
        P(None, "tp"),
        P("tp", None),
    )
    return jax.shard_map(
        local, mesh=mesh, in_specs=placed, out_specs=P(("dp", "ctx"), "tp"), check_vma=False
    )
```

time: 109 us -> 98.9 us (0.907)
  blocking collectives: 17.4 us -> 34.8 us
  local copies, waits for them, and re-layouts: 17.5 us -> 4.94 us
  waiting for transfers between devices: 30.1 us -> 24.1 us
  starting transfers between devices: 19.7 us -> 16.3 us
  other arithmetic: 4.55 us -> 1.36 us
  Pallas kernels: 18 us -> 15.6 us
    all_to_all x1 -> x2, blocking collectives: 17.4 us -> 34.8 us  [the longest x1 17.6 us: local(): parts = lax.all_to_all(sent.reshape(CTX, share, -1), 'ctx', 0, 0)]
    unnamed x12 -> x14, local copies, waits for them, and re-layouts: 15.7 us -> 4.91 us
    all_to_all x1 -> x0, waiting for transfers between devices: 5.54 us -> none  [local(): lax.all_to_all(jnp.broadcast_to(qkv[None, :, :width], (CTX, share, width)...]
    all_to_all x1 -> x0, starting transfers between devices: 3.65 us -> none  [local(): lax.all_to_all(jnp.broadcast_to(qkv[None, :, :width], (CTX, share, width)...]
    transpose x2 -> x1, other arithmetic: 3.87 us -> 0.69 us  [local(): values = jnp.where(visible, doc_values, 0).transpose(1, 0, 2)]
    ppermute x6, waiting for transfers between devices: 10.5 us -> 7.73 us  [shift(): return lax.ppermute(x, 'tp', [(i, (i + s) % TP) for i in range(TP)])]
    all_to_all x1, waiting for transfers between devices: 14 us -> 16.4 us  [local(): chunks = lax.all_to_all(response[0].reshape(CTX, share, feats), 'ctx', 0, 0)]
    broadcast_in_dim x2 -> x1, local copies, waits for them, and re-layouts: 1.76 us -> 0.01 us  [local(): keys = jnp.where(visible, doc_keys, doc_keys[:1]).transpose(1, 0, 2)]
  transfers between devices with their start and end apart: 8 -> 7, of which waited for: 8 -> 6; matrix products, arithmetic and copies ran while one was open for 10% -> 1% of each run, Pallas kernels for 0% -> 0%
where the time goes in v2:
time: 98.9 us; the launch traced here: 98.6 us
  blocking collectives  34.8 us (35%)
  waiting for transfers between devices  24.1 us (24%)
  starting transfers between devices  16.3 us (16%)
  Pallas kernels  15.6 us (16%)
  local copies, waits for them, and re-layouts  4.94 us (5%)
  between operations  1.38 us (1%)
  other arithmetic  1.36 us (1%)
    all_to_all x1, blocking collectives, local(): parts = lax.all_to_all(sent.reshape(CTX, share, -1), 'ctx', 0, 0)  17.6 us
    all_to_all x1, blocking collectives, local(): queries = lax.all_to_all(queries, 'ctx', 0, 0).reshape(count, -1)  17.3 us
    all_to_all x1, waiting for transfers between devices, local(): chunks = lax.all_to_all(response[0].reshape(CTX, share, feats), 'ctx', 0, 0)  16.4 us
    pallas_call x1, Pallas kernels, attend(): pl.pallas_call(functools.partial(attend_kernel, rows=rows, chunk=chunk),...  10.8 us
    all_to_all x1, starting transfers between devices, local(): chunks = lax.all_to_all(response[0].reshape(CTX, share, feats), 'ctx', 0, 0)  8.26 us
    ppermute x6, starting transfers between devices, shift(): return lax.ppermute(x, 'tp', [(i, (i + s) % TP) for i in range(TP)])  8.05 us
    ppermute x6, waiting for transfers between devices, shift(): return lax.ppermute(x, 'tp', [(i, (i + s) % TP) for i in range(TP)])  7.73 us
    unnamed x14, local copies, waits for them, and re-layouts  4.91 us
  transfers between devices with their start and end apart: 7, of which 6 were waited for; matrix products, arithmetic and copies ran while one was open for 1% of the time, Pallas kernels for 0%

profile of v2, /device:TPU:0, one launch (start us, length us, event | category | flops | bytes accessed | tf_op | source)
XLA Modules:
  0.0 98.6 jit_solution(5147266581190877942)
XLA Ops:
  0.0 0.0 copy-start.3
  0.0 0.0 copy-start.4
  0.0 8.3 %all-to-all-start = ((bf16[16,32,1024]{2,1,0:T(8,128)(2,1)}), bf16[16,32,1024]{2,1,0:T(8,128)(2,1)S(1)}, u32[]{:S(2)}, u32[]{:S(2)}) async-start(bf16[16,32,1024]{2,1,0:T(8,128)(2,1)} %bitcast.32), calls=%async_computation | async-start | bytes 2097152 | tf_op jit(solution)/shard_map/all_to_all | solution.py:194
  9.6 16.4 %all-to-all-done = bf16[16,32,1024]{2,1,0:T(8,128)(2,1)S(1)} async-done(((bf16[16,32,1024]{2,1,0:T(8,128)(2,1)}), bf16[16,32,1024]{2,1,0:T(8,128)(2,1)S(1)}, u32[]{:S(2)}, u32[]{:S(2)}) %all-to-all-start) | async-done | bytes 1048608 | tf_op jit(solution)/shard_map/all_to_all | solution.py:194
  26.0 2.8 %collective-permute-start.2 = (bf16[32,1024]{1,0:T(8,128)(2,1)S(1)}, bf16[32,1024]{1,0:T(8,128)(2,1)S(1)}, u32[]{:S(2)}, u32[]{:S(2)}) collective-permute-start(bf16[32,1024]{1,0:T(8,128)(2,1)S(1)} %dynamic-slice_bitcast_fusion.h.h0), channel_id=1, source_target_pairs={{0,3},{1,0},{2,1},{3,2},{4,7},{5,4},{6,5},{7,6},{8,11},{9,8},{10,9... | collective-permute-start | bytes 196616 | tf_op jit(solution)/shard_map/ppermute | solution.py:187
  28.7 0.8 collective-permute-start.1
  29.5 0.9 collective-permute-start
  30.4 0.0 copy-done.4
  30.4 0.0 copy-done.3
  30.4 0.0 copy-start
  30.4 0.0 copy-start.1
  30.5 0.7 fusion
  31.1 0.9 copy-done
  32.0 0.6 copy-done.1
  32.7 0.0 slice-start
  32.7 0.3 shard_map.91
  32.9 0.0 collective-permute-done.2.h3
  32.9 1.6 %collective-permute-done.1.h2 = bf16[32,1024]{1,0:T(8,128)(2,1)S(1)} collective-permute-done((bf16[32,1024]{1,0:T(8,128)(2,1)S(1)}, bf16[32,1024]{1,0:T(8,128)(2,1)S(1)}, u32[]{:S(2)}, u32[]{:S(2)}) %collective-permute-start.1) | collective-permute-done | bytes 65568 | tf_op jit(solution)/shard_map/ppermute | solution.py:187
  34.5 0.7 collective-permute-done.h1
  35.2 0.0 copy-start.2
  35.2 3.4 %copy-done.2 = bf16[4096,1024]{1,0:T(8,128)(2,1)S(1)} copy-done((bf16[4096,1024]{1,0:T(8,128)(2,1)S(1)}, bf16[4096,1024]{1,0:T(8,128)(2,1)}, u32[]{:S(2)}) %copy-start.2) | copy-done | bytes 8388632
  38.6 0.0 slice-start.1
  38.6 2.1 %shard_map.92 = (bf16[16,32,1024]{2,1,0:T(8,128)(2,1)S(1)}, bf16[32,256]{1,0:T(8,128)(2,1)S(1)}, bf16[32,256]{1,0:T(8,128)(2,1)S(1)}) custom-call(bf16[32,1024]{1,0:T(8,128)(2,1)S(1)} %dynamic-slice_bitcast_fusion.h.h0, bf16[32,1024]{1,0:T(8,128)(2,1)S(1)} %collective-permute-done.h1, bf16[32,1024]{1,0:T(8,128)(2,1)S(1)} %collective-permute-done.1.h2, ...), custom_call_target="tpu_custom_call" | custom-call | tf_op jit(solution)/shard_map/pallas_call | solution.py:65
  40.7 17.3 %all_to_all.15 = bf16[16,32,1024]{2,1,0:T(8,128)(2,1)S(1)} all-to-all(bf16[16,32,1024]{2,1,0:T(8,128)(2,1)S(1)} %get-tuple-element.32), channel_id=1, replica_groups=mesh['dp'=2,'ctx'=16,'tp'=4] {'ctx'}, dimensions={0} | all-to-all | bytes 2097152 | tf_op jit(solution)/shard_map/all_to_all | solution.py:208
  58.0 10.8 %shard_map.93 = bf16[512,1152]{1,0:T(8,128)(2,1)S(1)} custom-call(s32[1]{0:T(128)} %copy.19.len_ref, bf16[512,1024]{1,0:T(8,128)(2,1)S(1)} %bitcast.31, bf16[2,2048,128]{2,1,0:T(8,128)(2,1)S(1)} %get-tuple-element.33.k, bf16[2,2048,128]{2,1,0:T(8,128)(2,1)S(1)} %get-tuple-element.34.v, bf16[32,256]{1,0:T(8,128)(2,1)S(1)} %get-tuple-element.35.ks, ...), custom_call_target="tpu_custom_call" | custom-call | bytes 33554432 | tf_op jit(solution)/shard_map/pallas_call | solution.py:140
  68.8 17.6 %all_to_all.16.parts = bf16[16,32,1152]{2,1,0:T(8,128)(2,1)S(1)} all-to-all(bf16[16,32,1152]{2,1,0:T(8,128)(2,1)S(1)} %bitcast.30), channel_id=1, replica_groups=mesh['dp'=2,'ctx'=16,'tp'=4] {'ctx'}, dimensions={0} | all-to-all | bytes 2359296 | tf_op jit(solution)/shard_map/all_to_all | solution.py:210
  86.3 0.0 slice-done
  86.3 0.0 slice-done.1
  86.3 2.5 %shard_map.94 = bf16[4,32,1024]{2,1,0:T(8,128)(2,1)S(1)} custom-call(bf16[16,32,1152]{2,1,0:T(8,128)(2,1)S(1)} %all_to_all.16.parts, bf16[1024,4096]{1,0:T(8,128)(2,1)S(1)} %bitcast.29), custom_call_target="tpu_custom_call" | custom-call | flops 268435456 | bytes 8388608 | tf_op jit(solution)/shard_map/pallas_call | solution.py:174
  88.8 0.9 collective-permute-start.3
  89.7 2.4 %collective-permute-start.5 = (bf16[32,1024]{1,0:T(8,128)(2,1)S(1)}, bf16[32,1024]{1,0:T(8,128)(2,1)S(1)}, u32[]{:S(2)}, u32[]{:S(2)}) collective-permute-start(bf16[32,1024]{1,0:T(8,128)(2,1)S(1)} %get-tuple-element.38), channel_id=1, source_target_pairs={{0,3},{1,0},{2,1},{3,2},{4,7},{5,4},{6,5},{7,6},{8,11},{9,8},{10,9... | collective-permute-start | bytes 196616 | tf_op jit(solution)/shard_map/ppermute | solution.py:187
  92.1 0.3 collective-permute-start.4
  92.4 1.9 %collective-permute-done.3 = bf16[32,1024]{1,0:T(8,128)(2,1)S(1)} collective-permute-done((bf16[32,1024]{1,0:T(8,128)(2,1)S(1)}, bf16[32,1024]{1,0:T(8,128)(2,1)S(1)}, u32[]{:S(2)}, u32[]{:S(2)}) %collective-permute-start.3) | collective-permute-done | bytes 65568 | tf_op jit(solution)/shard_map/ppermute | solution.py:187
  94.4 0.3 collective-permute-done.5
  94.7 3.3 %collective-permute-done.4 = bf16[32,1024]{1,0:T(8,128)(2,1)S(1)} collective-permute-done((bf16[32,1024]{1,0:T(8,128)(2,1)S(1)}, bf16[32,1024]{1,0:T(8,128)(2,1)S(1)}, u32[]{:S(2)}, u32[]{:S(2)}) %collective-permute-start.4) | collective-permute-done | bytes 65568 | tf_op jit(solution)/shard_map/ppermute | solution.py:187
  97.9 0.7 fusion.4
  (5 shorter events, 0.0 us)
Async XLA Ops:
  0.0 30.4 %copy-start.3 = (bf16[2048,2,128]{2,1,0:T(2,128)(2,1)S(1)}, bf16[2048,2,128]{2,1,0:T(2,128)(2,1)}, u32[]{:S(2)}) copy-start(bf16[2048,2,128]{2,1,0:T(2,128)(2,1)} %param.13) | copy-start | bytes 3145732
  0.0 30.4 %copy-start.4 = (bf16[2048,2,128]{2,1,0:T(2,128)(2,1)S(1)}, bf16[2048,2,128]{2,1,0:T(2,128)(2,1)}, u32[]{:S(2)}) copy-start(bf16[2048,2,128]{2,1,0:T(2,128)(2,1)} %param.12) | copy-start | bytes 3145732
  0.0 26.0 %all-to-all-start = ((bf16[16,32,1024]{2,1,0:T(8,128)(2,1)}), bf16[16,32,1024]{2,1,0:T(8,128)(2,1)S(1)}, u32[]{:S(2)}, u32[]{:S(2)}) async-start(bf16[16,32,1024]{2,1,0:T(8,128)(2,1)} %bitcast.32), calls=%async_computation | async-start | bytes 2097152 | tf_op jit(solution)/shard_map/all_to_all | solution.py:194
  26.0 7.0 %collective-permute-start.2 = (bf16[32,1024]{1,0:T(8,128)(2,1)S(1)}, bf16[32,1024]{1,0:T(8,128)(2,1)S(1)}, u32[]{:S(2)}, u32[]{:S(2)}) collective-permute-start(bf16[32,1024]{1,0:T(8,128)(2,1)S(1)} %dynamic-slice_bitcast_fusion.h.h0), channel_id=1, source_target_pairs={{0,3},{1,0},{2,1},{3,2},{4,7},{5,4},{6,5},{7,6},{8,11},{9,8},{10,9... | collective-permute-start | bytes 196616 | tf_op jit(solution)/shard_map/ppermute | solution.py:187
  28.7 5.8 %collective-permute-start.1 = (bf16[32,1024]{1,0:T(8,128)(2,1)S(1)}, bf16[32,1024]{1,0:T(8,128)(2,1)S(1)}, u32[]{:S(2)}, u32[]{:S(2)}) collective-permute-start(bf16[32,1024]{1,0:T(8,128)(2,1)S(1)} %dynamic-slice_bitcast_fusion.h.h0), channel_id=1, source_target_pairs={{0,2},{1,3},{2,0},{3,1},{4,6},{5,7},{6,4},{7,5},{8,10},{9,11},{10,... | collective-permute-start | bytes 196616 | tf_op jit(solution)/shard_map/ppermute | solution.py:187
  29.5 5.7 %collective-permute-start = (bf16[32,1024]{1,0:T(8,128)(2,1)S(1)}, bf16[32,1024]{1,0:T(8,128)(2,1)S(1)}, u32[]{:S(2)}, u32[]{:S(2)}) collective-permute-start(bf16[32,1024]{1,0:T(8,128)(2,1)S(1)} %dynamic-slice_bitcast_fusion.h.h0), channel_id=1, source_target_pairs={{0,1},{1,2},{2,3},{3,0},{4,5},{5,6},{6,7},{7,4},{8,9},{9,10},{10,1... | collective-permute-start | bytes 196616 | tf_op jit(solution)/shard_map/ppermute | solution.py:187
  30.4 1.6 %copy-start = (bf16[4096,256]{1,0:T(8,128)(2,1)S(1)}, bf16[4096,256]{1,0:T(8,128)(2,1)}, u32[]{:S(2)}) copy-start(bf16[4096,256]{1,0:T(8,128)(2,1)} %wk.3) | copy-start | bytes 6291460
  30.4 2.2 %copy-start.1 = (bf16[4096,256]{1,0:T(8,128)(2,1)S(1)}, bf16[4096,256]{1,0:T(8,128)(2,1)}, u32[]{:S(2)}) copy-start(bf16[4096,256]{1,0:T(8,128)(2,1)} %wv.3) | copy-start | bytes 6291460
  32.7 53.7 %slice-start = ((s8[8388608]{0:T(1024)(128)(4,1)}), s8[4194304]{0:T(1024)(128)(4,1)S(1)}, s32[]{:S(2)}) async-start(s8[8388608]{0:T(1024)(128)(4,1)} %bitcast.28), calls=%async_computation.3 | async-start | bytes 8388608
  35.2 3.4 %copy-start.2 = (bf16[4096,1024]{1,0:T(8,128)(2,1)S(1)}, bf16[4096,1024]{1,0:T(8,128)(2,1)}, u32[]{:S(2)}) copy-start(bf16[4096,1024]{1,0:T(8,128)(2,1)} %wq.1) | copy-start | bytes 25165828
  38.6 47.8 %slice-start.1 = ((s8[8388608]{0:T(1024)(128)(4,1)}), s8[4194304]{0:T(1024)(128)(4,1)S(1)}, s32[]{:S(2)}) async-start(s8[8388608]{0:T(1024)(128)(4,1)} %bitcast.28), calls=%async_computation.4 | async-start | bytes 8388608
  88.8 5.5 %collective-permute-start.3 = (bf16[32,1024]{1,0:T(8,128)(2,1)S(1)}, bf16[32,1024]{1,0:T(8,128)(2,1)S(1)}, u32[]{:S(2)}, u32[]{:S(2)}) collective-permute-start(bf16[32,1024]{1,0:T(8,128)(2,1)S(1)} %get-tuple-element.37), channel_id=1, source_target_pairs={{0,1},{1,2},{2,3},{3,0},{4,5},{5,6},{6,7},{7,4},{8,9},{9,10},{10,1... | collective-permute-start | bytes 196616 | tf_op jit(solution)/shard_map/ppermute | solution.py:187
  89.7 4.9 %collective-permute-start.5 = (bf16[32,1024]{1,0:T(8,128)(2,1)S(1)}, bf16[32,1024]{1,0:T(8,128)(2,1)S(1)}, u32[]{:S(2)}, u32[]{:S(2)}) collective-permute-start(bf16[32,1024]{1,0:T(8,128)(2,1)S(1)} %get-tuple-element.38), channel_id=1, source_target_pairs={{0,3},{1,0},{2,1},{3,2},{4,7},{5,4},{6,5},{7,6},{8,11},{9,8},{10,9... | collective-permute-start | bytes 196616 | tf_op jit(solution)/shard_map/ppermute | solution.py:187
  92.1 5.8 %collective-permute-start.4 = (bf16[32,1024]{1,0:T(8,128)(2,1)S(1)}, bf16[32,1024]{1,0:T(8,128)(2,1)S(1)}, u32[]{:S(2)}, u32[]{:S(2)}) collective-permute-start(bf16[32,1024]{1,0:T(8,128)(2,1)S(1)} %get-tuple-element.39), channel_id=1, source_target_pairs={{0,2},{1,3},{2,0},{3,1},{4,6},{5,7},{6,4},{7,5},{8,10},{9,11},{10,... | collective-permute-start | bytes 196616 | tf_op jit(solution)/shard_map/ppermute | solution.py:187

commit v3 on v2

--- a/solution.py
+++ b/solution.py
@@ -23,23 +23,23 @@
     return lax.dot_general(a, b, (((1,), (1,)), ((), ())), preferred_element_type=f32)
 
 
-def begin_kernel(h, wk, wv, keys, values):
+def begin_kernel(h, wk, wv, ready, keys, values):
     feats = h.shape[1]
     start = pl.multiple_of(lax.axis_index("tp") * feats, feats)
     for w, out in ((wk, keys), (wv, values)):
         out[...] = dot(h[...], w[pl.ds(start, feats), :])
 
 
-def begin(mine, w_key, w_value):
+def begin(mine, w_key, w_value, ready):
     vmem = pl.BlockSpec(memory_space=pltpu.VMEM)
     return pl.pallas_call(
         begin_kernel,
-        in_specs=[vmem] * 3,
+        in_specs=[vmem] * 3 + [pl.BlockSpec(memory_space=pl.ANY)],
         out_specs=[vmem] * 2,
         out_shape=[jax.ShapeDtypeStruct((mine.shape[0], w.shape[1]), f32) for w in (w_key, w_value)],
         compiler_params=pltpu.CompilerParams(vmem_limit_bytes=6 * 2**20),
         cost_estimate=pl.CostEstimate(flops=0, bytes_accessed=48 * 2**20, transcendentals=0),
-    )(mine, w_key, w_value)
+    )(mine, w_key, w_value, ready)
 
 
 def project_kernel(h0, h1, h2, h3, k0, v0, wq, wk, wv, queries, keys, values):
@@ -147,10 +147,8 @@
     )(length, q, k, v, ks, vs)
 
 
-def finish_kernel(parts, w, out):
+def finish_kernel(parts, w, *outs, shifts):
     scale = (HEAD ** -0.5) * math.log2(math.e)
-    block = out.shape[2]
-    starts = [pl.multiple_of(lax.rem(lax.axis_index("tp") + s, TP) * block, block) for s in range(TP)]
     side = [parts[p, :, 8 * HEAD : 9 * HEAD].astype(f32) for p in range(CTX)]
     tops = [s[:, 0:8] + s[:, 8:16] + s[:, 16:24] for s in side]
     sums = [s[:, 24:32] + s[:, 32:40] + s[:, 40:48] for s in side]
@@ -162,23 +160,24 @@
         acc = sum(parts[p, :, h * HEAD : (h + 1) * HEAD].astype(f32) * scales[p][:, h : h + 1] for p in range(CTX))
         heads.append((acc / total[:, h : h + 1]).astype(bf16))
     attended = jnp.concatenate(heads, 1)
-    for s in range(TP):
-        out[s] = dot(attended, w[:, pl.ds(starts[s], block)]).astype(bf16)
-
-
-def finish(parts, w_out):
-    _, share, width = parts.shape
-    feats, cols = w_out.shape
-    block = cols // TP
-    vmem = pl.BlockSpec(memory_space=pltpu.VMEM)
-    return pl.pallas_call(
-        finish_kernel,
-        in_specs=[vmem, vmem],
-        out_specs=vmem,
-        out_shape=jax.ShapeDtypeStruct((TP, share, block), bf16),
+    block = outs[0].shape[1]
+    for s, out in zip(shifts, outs):
+        start = pl.multiple_of(lax.rem(lax.axis_index("tp") + s, TP) * block, block)
+        out[...] = dot(attended, w[:, pl.ds(start, block)]).astype(bf16)
+
+
+def finish(parts, w_out, shifts):
+    share = parts.shape[1]
+    block = w_out.shape[1] // TP
+    vmem = pl.BlockSpec(memory_space=pltpu.VMEM)
+    return pl.pallas_call(
+        functools.partial(finish_kernel, shifts=shifts),
+        in_specs=[vmem] * 2,
+        out_specs=[vmem] * len(shifts),
+        out_shape=[jax.ShapeDtypeStruct((share, block), bf16) for _ in shifts],
         compiler_params=pltpu.CompilerParams(vmem_limit_bytes=6 * 2**20),
         cost_estimate=pl.CostEstimate(
-            flops=2 * share * feats * cols, bytes_accessed=2 * w_out.size, transcendentals=0
+            flops=2 * share * w_out.size, bytes_accessed=2 * w_out.size, transcendentals=0
         ),
     )(parts, w_out)
 
@@ -200,7 +199,7 @@
     visible = (jnp.arange(cache) < doc_lengths[0])[:, None, None]
     keys = jnp.where(visible, doc_keys, doc_keys[:1]).transpose(1, 0, 2)
     values = jnp.where(visible, doc_values, 0).transpose(1, 0, 2)
-    begun = begin(mine, w_key, w_value)
+    begun = begin(mine, w_key, w_value, keys)
     queries, self_keys, self_values = project(pieces, begun, w_query, w_key, w_value)
     queries, keys, values, self_keys, self_values, doc_lengths = lax.optimization_barrier(
         (queries, keys, values, self_keys, self_values, doc_lengths)
@@ -208,11 +207,9 @@
     queries = lax.all_to_all(queries, "ctx", 0, 0).reshape(count, -1)
     sent = attend(doc_lengths, queries, keys, values, self_keys, self_values)
     parts = lax.all_to_all(sent.reshape(CTX, share, -1), "ctx", 0, 0)
-    partial_out = finish(parts, w_out)
-    out = partial_out[0].astype(f32)
-    for s in range(1, TP):
-        out += shift(partial_out[s], s).astype(f32)
-    return out.astype(bf16)
+    *away, own = finish(parts, w_out, (2, 1, 3, 0))
+    away = [shift(x, s) for x, s in zip(away, (2, 1, 3))]
+    return sum(x.astype(f32) for x in (own, *away)).astype(bf16)
 
 
 def solution(mesh):

time: 98.9 us -> 96.3 us (0.974)
  waiting for transfers between devices: 24.1 us -> 18.6 us
  starting transfers between devices: 16.3 us -> 18.4 us
  local copies, waits for them, and re-layouts: 4.94 us -> 2.93 us
  other arithmetic: 1.36 us -> 2.72 us
  blocking collectives: 34.8 us -> 35.9 us
    ppermute x6, waiting for transfers between devices: 7.73 us -> 2.25 us  [shift(): return lax.ppermute(x, 'tp', [(i, (i + s) % TP) for i in range(TP)])]
    unnamed x14 -> x10, local copies, waits for them, and re-layouts: 4.91 us -> 2.27 us
    ppermute x6, starting transfers between devices: 8.05 us -> 10.1 us  [shift(): return lax.ppermute(x, 'tp', [(i, (i + s) % TP) for i in range(TP)])]
    transpose x1, other arithmetic: 0.69 us -> 2.04 us  [local(): values = jnp.where(visible, doc_values, 0).transpose(1, 0, 2)]
  transfers between devices with their start and end apart: 7 -> 7, of which waited for: 6 -> 3; matrix products, arithmetic and copies ran while one was open for 1% -> 3% of each run, Pallas kernels for 0% -> 0%
where the time goes in v3:
time: 96.3 us; the launch traced here: 95.6 us
  blocking collectives  35.9 us (37%)
  waiting for transfers between devices  18.6 us (19%)
  starting transfers between devices  18.4 us (19%)
  Pallas kernels  15.6 us (16%)
  local copies, waits for them, and re-layouts  2.93 us (3%)
  other arithmetic  2.72 us (3%)
  between operations  1.39 us (1%)
    all_to_all x1, blocking collectives, local(): parts = lax.all_to_all(sent.reshape(CTX, share, -1), 'ctx', 0, 0)  18.1 us
    all_to_all x1, blocking collectives, local(): queries = lax.all_to_all(queries, 'ctx', 0, 0).reshape(count, -1)  17.8 us
    all_to_all x1, waiting for transfers between devices, local(): chunks = lax.all_to_all(response[0].reshape(CTX, share, feats), 'ctx', 0, 0)  16.4 us
    pallas_call x1, Pallas kernels, attend(): pl.pallas_call(functools.partial(attend_kernel, rows=rows, chunk=chunk),...  10.8 us
    ppermute x6, starting transfers between devices, shift(): return lax.ppermute(x, 'tp', [(i, (i + s) % TP) for i in range(TP)])  10.1 us
    all_to_all x1, starting transfers between devices, local(): chunks = lax.all_to_all(response[0].reshape(CTX, share, feats), 'ctx', 0, 0)  8.26 us
    pallas_call x1, Pallas kernels, finish(): pl.pallas_call(functools.partial(finish_kernel, shifts=shifts), in_specs=...  2.46 us
    unnamed x10, local copies, waits for them, and re-layouts  2.27 us
  transfers between devices with their start and end apart: 7, of which 3 were waited for; matrix products, arithmetic and copies ran while one was open for 3% of the time, Pallas kernels for 0%

profile of v3, /device:TPU:0, one launch (start us, length us, event | category | flops | bytes accessed | tf_op | source)
XLA Modules:
  0.0 95.6 jit_solution(12050299445571202144)
XLA Ops:
  0.0 0.0 copy-start.1
  0.0 8.3 %all-to-all-start = ((bf16[16,32,1024]{2,1,0:T(8,128)(2,1)}), bf16[16,32,1024]{2,1,0:T(8,128)(2,1)S(1)}, u32[]{:S(2)}, u32[]{:S(2)}) async-start(bf16[16,32,1024]{2,1,0:T(8,128)(2,1)} %bitcast.21), calls=%async_computation | async-start | bytes 2097152 | tf_op jit(solution)/shard_map/all_to_all | solution.py:193
  9.6 16.4 %all-to-all-done = bf16[16,32,1024]{2,1,0:T(8,128)(2,1)S(1)} async-done(((bf16[16,32,1024]{2,1,0:T(8,128)(2,1)}), bf16[16,32,1024]{2,1,0:T(8,128)(2,1)S(1)}, u32[]{:S(2)}, u32[]{:S(2)}) %all-to-all-start) | async-done | bytes 1048608 | tf_op jit(solution)/shard_map/all_to_all | solution.py:193
  26.0 2.8 %collective-permute-start.2 = (bf16[32,1024]{1,0:T(8,128)(2,1)S(1)}, bf16[32,1024]{1,0:T(8,128)(2,1)S(1)}, u32[]{:S(2)}, u32[]{:S(2)}) collective-permute-start(bf16[32,1024]{1,0:T(8,128)(2,1)S(1)} %dynamic-slice_bitcast_fusion.h.h0), channel_id=1, source_target_pairs={{0,3},{1,0},{2,1},{3,2},{4,7},{5,4},{6,5},{7,6},{8,11},{9,8},{10,9... | collective-permute-start | bytes 196616 | tf_op jit(solution)/shard_map/ppermute | solution.py:186
  28.7 0.8 collective-permute-start.1
  29.5 0.9 collective-permute-start
  30.4 0.7 slice_bitcast_fusion
  31.1 0.0 copy-start
  31.1 2.0 %fusion = (bf16[2,2048,128]{2,1,0:T(8,128)(2,1)S(1)}, bf16[2,2048,128]{2,1,0:T(8,128)(2,1)S(1)}) fusion(bf16[2048,2,128]{2,1,0:T(2,128)(2,1)} %param.13, pred[2048]{0:T(1024)(128)(4,1)S(1)} %iota_compare_fusion, bf16[2,128]{1,0:T(2,128)(2,1)S(1)} %slice_bitcast_fusion, bf16[2048,2,128]{2,1,0:T(2,128)(2,1)} %param.12), kind=kLoop, calls=%fused_computation.1 | loop fusion | flops 1048576 | bytes 4196864 | tf_op jit(solution)/shard_map/transpose | solution.py:201
  33.1 0.0 copy-done.1
  33.1 0.0 copy-start.2
  33.2 2.0 %copy-done.2 = bf16[4096,256]{1,0:T(8,128)(2,1)S(1)} copy-done((bf16[4096,256]{1,0:T(8,128)(2,1)S(1)}, bf16[4096,256]{1,0:T(8,128)(2,1)}, u32[]{:S(2)}) %copy-start.2) | copy-done | bytes 2097176
  35.1 0.0 slice-start
  35.1 0.3 shard_map.91
  35.4 0.0 collective-permute-done.2.h3
  35.4 0.0 collective-permute-done.1.h2
  35.4 0.0 collective-permute-done.h1
  35.4 0.3 copy-done
  35.7 0.0 slice-start.1
  35.7 2.1 %shard_map.92 = (bf16[16,32,1024]{2,1,0:T(8,128)(2,1)S(1)}, bf16[32,256]{1,0:T(8,128)(2,1)S(1)}, bf16[32,256]{1,0:T(8,128)(2,1)S(1)}) custom-call(bf16[32,1024]{1,0:T(8,128)(2,1)S(1)} %dynamic-slice_bitcast_fusion.h.h0, bf16[32,1024]{1,0:T(8,128)(2,1)S(1)} %collective-permute-done.h1, bf16[32,1024]{1,0:T(8,128)(2,1)S(1)} %collective-permute-done.1.h2, ...), custom_call_target="tpu_custom_call" | custom-call | tf_op jit(solution)/shard_map/pallas_call | solution.py:65
  37.8 17.8 %all_to_all.15 = bf16[16,32,1024]{2,1,0:T(8,128)(2,1)S(1)} all-to-all(bf16[16,32,1024]{2,1,0:T(8,128)(2,1)S(1)} %get-tuple-element.36), channel_id=1, replica_groups=mesh['dp'=2,'ctx'=16,'tp'=4] {'ctx'}, dimensions={0} | all-to-all | bytes 2097152 | tf_op jit(solution)/shard_map/all_to_all | solution.py:207
  55.7 10.8 %shard_map.93 = bf16[512,1152]{1,0:T(8,128)(2,1)S(1)} custom-call(s32[1]{0:T(128)} %copy.19.len_ref, bf16[512,1024]{1,0:T(8,128)(2,1)S(1)} %bitcast.20, bf16[2,2048,128]{2,1,0:T(8,128)(2,1)S(1)} %get-tuple-element.37.ready.k, bf16[2,2048,128]{2,1,0:T(8,128)(2,1)S(1)} %get-tuple-element.38.v, bf16[32,256]{1,0:T(8,128)(2,1)S(1)} %get-tuple-element.39.ks, ...), custom_call_target="tpu_custom_call" | custom-call | bytes 33554432 | tf_op jit(solution)/shard_map/pallas_call | solution.py:140
  66.5 18.1 %all_to_all.16.parts = bf16[16,32,1152]{2,1,0:T(8,128)(2,1)S(1)} all-to-all(bf16[16,32,1152]{2,1,0:T(8,128)(2,1)S(1)} %bitcast.19), channel_id=1, replica_groups=mesh['dp'=2,'ctx'=16,'tp'=4] {'ctx'}, dimensions={0} | all-to-all | bytes 2359296 | tf_op jit(solution)/shard_map/all_to_all | solution.py:209
  84.6 0.0 slice-done
  84.6 0.0 slice-done.1
  84.6 2.5 %shard_map.94 = (bf16[32,1024]{1,0:T(8,128)(2,1)S(1)}, bf16[32,1024]{1,0:T(8,128)(2,1)S(1)}, bf16[32,1024]{1,0:T(8,128)(2,1)S(1)}, bf16[32,1024]{1,0:T(8,128)(2,1)S(1)}) custom-call(bf16[16,32,1152]{2,1,0:T(8,128)(2,1)S(1)} %all_to_all.16.parts, bf16[1024,4096]{1,0:T(8,128)(2,1)S(1)} %bitcast.18), custom_call_target="tpu_custom_call" | custom-call | flops 268435456 | bytes 8388608 | tf_op jit(solution)/shard_map/pallas_call | solution.py:173
  87.0 2.5 %collective-permute-start.3 = (bf16[32,1024]{1,0:T(8,128)(2,1)S(1)}, bf16[32,1024]{1,0:T(8,128)(2,1)S(1)}, u32[]{:S(2)}, u32[]{:S(2)}) collective-permute-start(bf16[32,1024]{1,0:T(8,128)(2,1)S(1)} %get-tuple-element.42), channel_id=1, source_target_pairs={{0,2},{1,3},{2,0},{3,1},{4,6},{5,7},{6,4},{7,5},{8,10},{9,11},{10,... | collective-permute-start | bytes 196616 | tf_op jit(solution)/shard_map/ppermute | solution.py:186
  89.5 0.8 collective-permute-start.4
  90.3 2.4 %collective-permute-start.5 = (bf16[32,1024]{1,0:T(8,128)(2,1)S(1)}, bf16[32,1024]{1,0:T(8,128)(2,1)S(1)}, u32[]{:S(2)}, u32[]{:S(2)}) collective-permute-start(bf16[32,1024]{1,0:T(8,128)(2,1)S(1)} %get-tuple-element.44), channel_id=1, source_target_pairs={{0,3},{1,0},{2,1},{3,2},{4,7},{5,4},{6,5},{7,6},{8,11},{9,8},{10,9... | collective-permute-start | bytes 196616 | tf_op jit(solution)/shard_map/ppermute | solution.py:186
  92.7 0.1 collective-permute-done.3
  92.8 2.1 %collective-permute-done.4 = bf16[32,1024]{1,0:T(8,128)(2,1)S(1)} collective-permute-done((bf16[32,1024]{1,0:T(8,128)(2,1)S(1)}, bf16[32,1024]{1,0:T(8,128)(2,1)S(1)}, u32[]{:S(2)}, u32[]{:S(2)}) %collective-permute-start.4) | collective-permute-done | bytes 65568 | tf_op jit(solution)/shard_map/ppermute | solution.py:186
  95.0 0.0 collective-permute-done.5
  95.0 0.7 add_convert_fusion
  (3 shorter events, 0.0 us)
Async XLA Ops:
  0.0 33.1 %copy-start.1 = (bf16[4096,256]{1,0:T(8,128)(2,1)S(1)}, bf16[4096,256]{1,0:T(8,128)(2,1)}, u32[]{:S(2)}) copy-start(bf16[4096,256]{1,0:T(8,128)(2,1)} %wk.3) | copy-start | bytes 6291460
  0.0 26.0 %all-to-all-start = ((bf16[16,32,1024]{2,1,0:T(8,128)(2,1)}), bf16[16,32,1024]{2,1,0:T(8,128)(2,1)S(1)}, u32[]{:S(2)}, u32[]{:S(2)}) async-start(bf16[16,32,1024]{2,1,0:T(8,128)(2,1)} %bitcast.21), calls=%async_computation | async-start | bytes 2097152 | tf_op jit(solution)/shard_map/all_to_all | solution.py:193
  26.0 9.4 %collective-permute-start.2 = (bf16[32,1024]{1,0:T(8,128)(2,1)S(1)}, bf16[32,1024]{1,0:T(8,128)(2,1)S(1)}, u32[]{:S(2)}, u32[]{:S(2)}) collective-permute-start(bf16[32,1024]{1,0:T(8,128)(2,1)S(1)} %dynamic-slice_bitcast_fusion.h.h0), channel_id=1, source_target_pairs={{0,3},{1,0},{2,1},{3,2},{4,7},{5,4},{6,5},{7,6},{8,11},{9,8},{10,9... | collective-permute-start | bytes 196616 | tf_op jit(solution)/shard_map/ppermute | solution.py:186
  28.7 6.7 %collective-permute-start.1 = (bf16[32,1024]{1,0:T(8,128)(2,1)S(1)}, bf16[32,1024]{1,0:T(8,128)(2,1)S(1)}, u32[]{:S(2)}, u32[]{:S(2)}) collective-permute-start(bf16[32,1024]{1,0:T(8,128)(2,1)S(1)} %dynamic-slice_bitcast_fusion.h.h0), channel_id=1, source_target_pairs={{0,2},{1,3},{2,0},{3,1},{4,6},{5,7},{6,4},{7,5},{8,10},{9,11},{10,... | collective-permute-start | bytes 196616 | tf_op jit(solution)/shard_map/ppermute | solution.py:186
  29.5 5.9 %collective-permute-start = (bf16[32,1024]{1,0:T(8,128)(2,1)S(1)}, bf16[32,1024]{1,0:T(8,128)(2,1)S(1)}, u32[]{:S(2)}, u32[]{:S(2)}) collective-permute-start(bf16[32,1024]{1,0:T(8,128)(2,1)S(1)} %dynamic-slice_bitcast_fusion.h.h0), channel_id=1, source_target_pairs={{0,1},{1,2},{2,3},{3,0},{4,5},{5,6},{6,7},{7,4},{8,9},{9,10},{10,1... | collective-permute-start | bytes 196616 | tf_op jit(solution)/shard_map/ppermute | solution.py:186
  31.1 4.6 %copy-start = (bf16[4096,1024]{1,0:T(8,128)(2,1)S(1)}, bf16[4096,1024]{1,0:T(8,128)(2,1)}, u32[]{:S(2)}) copy-start(bf16[4096,1024]{1,0:T(8,128)(2,1)} %wq.1) | copy-start | bytes 25165828
  33.1 2.0 %copy-start.2 = (bf16[4096,256]{1,0:T(8,128)(2,1)S(1)}, bf16[4096,256]{1,0:T(8,128)(2,1)}, u32[]{:S(2)}) copy-start(bf16[4096,256]{1,0:T(8,128)(2,1)} %wv.3) | copy-start | bytes 6291460
  35.1 49.5 %slice-start = ((s8[8388608]{0:T(1024)(128)(4,1)}), s8[4194304]{0:T(1024)(128)(4,1)S(1)}, s32[]{:S(2)}) async-start(s8[8388608]{0:T(1024)(128)(4,1)} %bitcast.17), calls=%async_computation.3 | async-start | bytes 8388608
  35.7 48.9 %slice-start.1 = ((s8[8388608]{0:T(1024)(128)(4,1)}), s8[4194304]{0:T(1024)(128)(4,1)S(1)}, s32[]{:S(2)}) async-start(s8[8388608]{0:T(1024)(128)(4,1)} %bitcast.17), calls=%async_computation.4 | async-start | bytes 8388608
  87.0 5.8 %collective-permute-start.3 = (bf16[32,1024]{1,0:T(8,128)(2,1)S(1)}, bf16[32,1024]{1,0:T(8,128)(2,1)S(1)}, u32[]{:S(2)}, u32[]{:S(2)}) collective-permute-start(bf16[32,1024]{1,0:T(8,128)(2,1)S(1)} %get-tuple-element.42), channel_id=1, source_target_pairs={{0,2},{1,3},{2,0},{3,1},{4,6},{5,7},{6,4},{7,5},{8,10},{9,11},{10,... | collective-permute-start | bytes 196616 | tf_op jit(solution)/shard_map/ppermute | solution.py:186
  89.5 5.5 %collective-permute-start.4 = (bf16[32,1024]{1,0:T(8,128)(2,1)S(1)}, bf16[32,1024]{1,0:T(8,128)(2,1)S(1)}, u32[]{:S(2)}, u32[]{:S(2)}) collective-permute-start(bf16[32,1024]{1,0:T(8,128)(2,1)S(1)} %get-tuple-element.43), channel_id=1, source_target_pairs={{0,1},{1,2},{2,3},{3,0},{4,5},{5,6},{6,7},{7,4},{8,9},{9,10},{10,1... | collective-permute-start | bytes 196616 | tf_op jit(solution)/shard_map/ppermute | solution.py:186
  90.3 4.7 %collective-permute-start.5 = (bf16[32,1024]{1,0:T(8,128)(2,1)S(1)}, bf16[32,1024]{1,0:T(8,128)(2,1)S(1)}, u32[]{:S(2)}, u32[]{:S(2)}) collective-permute-start(bf16[32,1024]{1,0:T(8,128)(2,1)S(1)} %get-tuple-element.44), channel_id=1, source_target_pairs={{0,3},{1,0},{2,1},{3,2},{4,7},{5,4},{6,5},{7,6},{8,11},{9,8},{10,9... | collective-permute-start | bytes 196616 | tf_op jit(solution)/shard_map/ppermute | solution.py:186

commit v4 on v3

--- a/solution.py
+++ b/solution.py
@@ -93,6 +93,12 @@
     counted = [
         jnp.where((chunk_at < len_ref[0] - c) & (chunk_lane == 0), 1.0, 0.0).astype(bf16) for c in starts
     ]
+    hidden = [jnp.where(chunk_at < len_ref[0] - c, 0.0, 1.0).astype(bf16) for c in starts]
+    fill = [[gone * k[kv, 0:1, :] for gone in hidden] for kv in range(2)]
+
+    def keys_of(kv, n):
+        block = k[kv, n * chunk : (n + 1) * chunk, :]
+        return block + fill[kv][n] if n else block
 
     def heads_of(r, kv):
         cols = [(kv * groups + g) * HEAD for g in range(groups)]
@@ -102,7 +108,7 @@
         return ref[:, kv * HEAD : (kv + 1) * HEAD]
 
     heads = heads_of(*units[0])
-    scores = [dot_nt(heads, k[0, c : c + chunk, :]) for c in starts]
+    scores = [dot_nt(heads, keys_of(0, n)) for n in range(len(starts))]
     for n, (r, kv) in enumerate(units):
         self_scores = jnp.where(key_at <= row_at + r, dot_nt(heads, of_kv(ks, kv)), -1e30)
         tops = [s[:, c : c + HEAD] for s in scores for c in range(0, chunk, HEAD)]
@@ -114,9 +120,9 @@
         if after:
             heads = heads_of(*after)
         upcoming = []
-        for c, s, count in zip(starts, scores, counted):
+        for m, (c, s, count) in enumerate(zip(starts, scores, counted)):
             if after:
-                upcoming.append(dot_nt(heads, k[after[1], c : c + chunk, :]))
+                upcoming.append(dot_nt(heads, keys_of(after[1], m)))
             acc += dot(weigh(s), jnp.concatenate([v[kv, c : c + chunk, :], count], 1))
         scores = upcoming
         if kv == 0:
@@ -155,15 +161,21 @@
     top = functools.reduce(jnp.maximum, tops)
     scales = [jnp.exp2((m - top) * scale) for m in tops]
     total = sum(a * b for a, b in zip(scales, sums))
-    heads = []
-    for h in range(8):
-        acc = sum(parts[p, :, h * HEAD : (h + 1) * HEAD].astype(f32) * scales[p][:, h : h + 1] for p in range(CTX))
-        heads.append((acc / total[:, h : h + 1]).astype(bf16))
-    attended = jnp.concatenate(heads, 1)
     block = outs[0].shape[1]
-    for s, out in zip(shifts, outs):
-        start = pl.multiple_of(lax.rem(lax.axis_index("tp") + s, TP) * block, block)
-        out[...] = dot(attended, w[:, pl.ds(start, block)]).astype(bf16)
+    starts = [pl.multiple_of(lax.rem(lax.axis_index("tp") + s, TP) * block, block) for s in shifts]
+    sums_out = [0.0] * len(shifts)
+    for first in range(0, 8, 2):
+        heads = []
+        for h in (first, first + 1):
+            acc = sum(
+                parts[p, :, h * HEAD : (h + 1) * HEAD].astype(f32) * scales[p][:, h : h + 1] for p in range(CTX)
+            )
+            heads.append((acc / total[:, h : h + 1]).astype(bf16))
+        attended = jnp.concatenate(heads, 1)
+        rows = pl.ds(first * HEAD, 2 * HEAD)
+        sums_out = [o + dot(attended, w[rows, pl.ds(c, block)]) for o, c in zip(sums_out, starts)]
+    for out, value in zip(outs, sums_out):
+        out[...] = value.astype(bf16)
 
 
 def finish(parts, w_out, shifts):
@@ -197,7 +209,7 @@
     mine = lax.dynamic_index_in_dim(chunks, owner[0], 0, keepdims=False)
     pieces = [mine] + [shift(mine, s) for s in range(1, TP)]
     visible = (jnp.arange(cache) < doc_lengths[0])[:, None, None]
-    keys = jnp.where(visible, doc_keys, doc_keys[:1]).transpose(1, 0, 2)
+    keys = jnp.where(visible, doc_keys, 0).transpose(1, 0, 2)
     values = jnp.where(visible, doc_values, 0).transpose(1, 0, 2)
     begun = begin(mine, w_key, w_value, keys)
     queries, self_keys, self_values = project(pieces, begun, w_query, w_key, w_value)

time: 96.3 us -> 95.3 us (0.990)
  transfers between devices with their start and end apart: 7 -> 7, of which waited for: 3 -> 3; matrix products, arithmetic and copies ran while one was open for 3% -> 2% of each run, Pallas kernels for 0% -> 0%
where the time goes in v4:
time: 95.3 us; the launch traced here: 94.6 us
  blocking collectives  35.6 us (37%)
  waiting for transfers between devices  19.1 us (20%)
  starting transfers between devices  18.6 us (20%)
  Pallas kernels  15.3 us (16%)
  other arithmetic  2.71 us (3%)
  local copies, waits for them, and re-layouts  1.98 us (2%)
  between operations  1.38 us (1%)
    all_to_all x1, blocking collectives, local(): parts = lax.all_to_all(sent.reshape(CTX, share, -1), 'ctx', 0, 0)  17.9 us
    all_to_all x1, blocking collectives, local(): queries = lax.all_to_all(queries, 'ctx', 0, 0).reshape(count, -1)  17.7 us
    all_to_all x1, waiting for transfers between devices, local(): chunks = lax.all_to_all(response[0].reshape(CTX, share, feats), 'ctx', 0, 0)  16.4 us
    pallas_call x1, Pallas kernels, attend(): pl.pallas_call(functools.partial(attend_kernel, rows=rows, chunk=chunk),...  10.8 us
    ppermute x6, starting transfers between devices, shift(): return lax.ppermute(x, 'tp', [(i, (i + s) % TP) for i in range(TP)])  10.3 us
    all_to_all x1, starting transfers between devices, local(): chunks = lax.all_to_all(response[0].reshape(CTX, share, feats), 'ctx', 0, 0)  8.26 us
    ppermute x6, waiting for transfers between devices, shift(): return lax.ppermute(x, 'tp', [(i, (i + s) % TP) for i in range(TP)])  2.71 us
    pallas_call x1, Pallas kernels, project(): pl.pallas_call(project_kernel, in_specs=[vmem] * 9, out_specs=[vmem] * 3,...  2.11 us
  transfers between devices with their start and end apart: 7, of which 3 were waited for; matrix products, arithmetic and copies ran while one was open for 2% of the time, Pallas kernels for 0%

profile of v4, /device:TPU:0, one launch (start us, length us, event | category | flops | bytes accessed | tf_op | source)
XLA Modules:
  0.0 94.6 jit_solution(13538792955199085974)
XLA Ops:
  0.0 0.0 copy-start.1
  0.0 8.3 %all-to-all-start = ((bf16[16,32,1024]{2,1,0:T(8,128)(2,1)}), bf16[16,32,1024]{2,1,0:T(8,128)(2,1)S(1)}, u32[]{:S(2)}, u32[]{:S(2)}) async-start(bf16[16,32,1024]{2,1,0:T(8,128)(2,1)} %bitcast.19), calls=%async_computation | async-start | bytes 2097152 | tf_op jit(solution)/shard_map/all_to_all | solution.py:205
  9.6 16.4 %all-to-all-done = bf16[16,32,1024]{2,1,0:T(8,128)(2,1)S(1)} async-done(((bf16[16,32,1024]{2,1,0:T(8,128)(2,1)}), bf16[16,32,1024]{2,1,0:T(8,128)(2,1)S(1)}, u32[]{:S(2)}, u32[]{:S(2)}) %all-to-all-start) | async-done | bytes 1048608 | tf_op jit(solution)/shard_map/all_to_all | solution.py:205
  26.0 2.8 %collective-permute-start.2 = (bf16[32,1024]{1,0:T(8,128)(2,1)S(1)}, bf16[32,1024]{1,0:T(8,128)(2,1)S(1)}, u32[]{:S(2)}, u32[]{:S(2)}) collective-permute-start(bf16[32,1024]{1,0:T(8,128)(2,1)S(1)} %dynamic-slice_bitcast_fusion.h.h0), channel_id=1, source_target_pairs={{0,3},{1,0},{2,1},{3,2},{4,7},{5,4},{6,5},{7,6},{8,11},{9,8},{10,9... | collective-permute-start | bytes 196616 | tf_op jit(solution)/shard_map/ppermute | solution.py:198
  28.7 0.8 collective-permute-start.1
  29.5 0.9 collective-permute-start
  30.4 0.0 copy-start
  30.4 2.0 %fusion = (bf16[2,2048,128]{2,1,0:T(8,128)(2,1)S(1)}, bf16[2,2048,128]{2,1,0:T(8,128)(2,1)S(1)}) fusion(bf16[2048,2,128]{2,1,0:T(2,128)(2,1)} %param.13, pred[2048]{0:T(1024)(128)(4,1)S(1)} %iota_compare_fusion, bf16[2048,2,128]{2,1,0:T(2,128)(2,1)} %param.12), kind=kLoop, calls=%fused_computation.1 | loop fusion | flops 1048576 | bytes 4196352 | tf_op jit(solution)/shard_map/transpose | solution.py:213
  32.5 0.0 copy-done.1
  32.5 0.0 copy-start.2
  32.5 2.0 %copy-done.2 = bf16[4096,256]{1,0:T(8,128)(2,1)S(1)} copy-done((bf16[4096,256]{1,0:T(8,128)(2,1)S(1)}, bf16[4096,256]{1,0:T(8,128)(2,1)}, u32[]{:S(2)}) %copy-start.2) | copy-done | bytes 2097176
  34.4 0.0 slice-start
  34.5 0.3 shard_map.91
  34.7 0.0 collective-permute-done.2.h3
  34.7 0.0 collective-permute-done.1.h2
  34.8 0.5 collective-permute-done.h1
  35.2 0.0 copy-done
  35.2 0.0 slice-start.1
  35.2 2.1 %shard_map.92 = (bf16[16,32,1024]{2,1,0:T(8,128)(2,1)S(1)}, bf16[32,256]{1,0:T(8,128)(2,1)S(1)}, bf16[32,256]{1,0:T(8,128)(2,1)S(1)}) custom-call(bf16[32,1024]{1,0:T(8,128)(2,1)S(1)} %dynamic-slice_bitcast_fusion.h.h0, bf16[32,1024]{1,0:T(8,128)(2,1)S(1)} %collective-permute-done.h1, bf16[32,1024]{1,0:T(8,128)(2,1)S(1)} %collective-permute-done.1.h2, ...), custom_call_target="tpu_custom_call" | custom-call | tf_op jit(solution)/shard_map/pallas_call | solution.py:65
  37.3 17.7 %all_to_all.15 = bf16[16,32,1024]{2,1,0:T(8,128)(2,1)S(1)} all-to-all(bf16[16,32,1024]{2,1,0:T(8,128)(2,1)S(1)} %get-tuple-element.36), channel_id=1, replica_groups=mesh['dp'=2,'ctx'=16,'tp'=4] {'ctx'}, dimensions={0} | all-to-all | bytes 2097152 | tf_op jit(solution)/shard_map/all_to_all | solution.py:219
  55.0 10.8 %shard_map.93 = bf16[512,1152]{1,0:T(8,128)(2,1)S(1)} custom-call(s32[1]{0:T(128)} %copy.19.len_ref, bf16[512,1024]{1,0:T(8,128)(2,1)S(1)} %bitcast.18, bf16[2,2048,128]{2,1,0:T(8,128)(2,1)S(1)} %get-tuple-element.37.ready.k, bf16[2,2048,128]{2,1,0:T(8,128)(2,1)S(1)} %get-tuple-element.38.v, bf16[32,256]{1,0:T(8,128)(2,1)S(1)} %get-tuple-element.39.ks, ...), custom_call_target="tpu_custom_call" | custom-call | bytes 33554432 | tf_op jit(solution)/shard_map/pallas_call | solution.py:146
  65.9 17.9 %all_to_all.16.parts = bf16[16,32,1152]{2,1,0:T(8,128)(2,1)S(1)} all-to-all(bf16[16,32,1152]{2,1,0:T(8,128)(2,1)S(1)} %bitcast.17), channel_id=1, replica_groups=mesh['dp'=2,'ctx'=16,'tp'=4] {'ctx'}, dimensions={0} | all-to-all | bytes 2359296 | tf_op jit(solution)/shard_map/all_to_all | solution.py:221
  83.8 0.0 slice-done
  83.8 0.0 slice-done.1
  83.8 2.1 %shard_map.94 = (bf16[32,1024]{1,0:T(8,128)(2,1)S(1)}, bf16[32,1024]{1,0:T(8,128)(2,1)S(1)}, bf16[32,1024]{1,0:T(8,128)(2,1)S(1)}, bf16[32,1024]{1,0:T(8,128)(2,1)S(1)}) custom-call(bf16[16,32,1152]{2,1,0:T(8,128)(2,1)S(1)} %all_to_all.16.parts, bf16[1024,4096]{1,0:T(8,128)(2,1)S(1)} %bitcast.16), custom_call_target="tpu_custom_call" | custom-call | flops 268435456 | bytes 8388608 | tf_op jit(solution)/shard_map/pallas_call | solution.py:185
  85.9 2.6 %collective-permute-start.3 = (bf16[32,1024]{1,0:T(8,128)(2,1)S(1)}, bf16[32,1024]{1,0:T(8,128)(2,1)S(1)}, u32[]{:S(2)}, u32[]{:S(2)}) collective-permute-start(bf16[32,1024]{1,0:T(8,128)(2,1)S(1)} %get-tuple-element.42), channel_id=1, source_target_pairs={{0,2},{1,3},{2,0},{3,1},{4,6},{5,7},{6,4},{7,5},{8,10},{9,11},{10,... | collective-permute-start | bytes 196616 | tf_op jit(solution)/shard_map/ppermute | solution.py:198
  88.5 0.8 collective-permute-start.4
  89.3 2.4 %collective-permute-start.5 = (bf16[32,1024]{1,0:T(8,128)(2,1)S(1)}, bf16[32,1024]{1,0:T(8,128)(2,1)S(1)}, u32[]{:S(2)}, u32[]{:S(2)}) collective-permute-start(bf16[32,1024]{1,0:T(8,128)(2,1)S(1)} %get-tuple-element.44), channel_id=1, source_target_pairs={{0,3},{1,0},{2,1},{3,2},{4,7},{5,4},{6,5},{7,6},{8,11},{9,8},{10,9... | collective-permute-start | bytes 196616 | tf_op jit(solution)/shard_map/ppermute | solution.py:198
  91.7 0.0 collective-permute-done.3
  91.7 2.2 %collective-permute-done.4 = bf16[32,1024]{1,0:T(8,128)(2,1)S(1)} collective-permute-done((bf16[32,1024]{1,0:T(8,128)(2,1)S(1)}, bf16[32,1024]{1,0:T(8,128)(2,1)S(1)}, u32[]{:S(2)}, u32[]{:S(2)}) %collective-permute-start.4) | collective-permute-done | bytes 65568 | tf_op jit(solution)/shard_map/ppermute | solution.py:198
  94.0 0.0 collective-permute-done.5
  94.0 0.7 add_convert_fusion
  (3 shorter events, 0.0 us)
Async XLA Ops:
  0.0 32.5 %copy-start.1 = (bf16[4096,256]{1,0:T(8,128)(2,1)S(1)}, bf16[4096,256]{1,0:T(8,128)(2,1)}, u32[]{:S(2)}) copy-start(bf16[4096,256]{1,0:T(8,128)(2,1)} %wk.3) | copy-start | bytes 6291460
  0.0 26.0 %all-to-all-start = ((bf16[16,32,1024]{2,1,0:T(8,128)(2,1)}), bf16[16,32,1024]{2,1,0:T(8,128)(2,1)S(1)}, u32[]{:S(2)}, u32[]{:S(2)}) async-start(bf16[16,32,1024]{2,1,0:T(8,128)(2,1)} %bitcast.19), calls=%async_computation | async-start | bytes 2097152 | tf_op jit(solution)/shard_map/all_to_all | solution.py:205
  26.0 8.8 %collective-permute-start.2 = (bf16[32,1024]{1,0:T(8,128)(2,1)S(1)}, bf16[32,1024]{1,0:T(8,128)(2,1)S(1)}, u32[]{:S(2)}, u32[]{:S(2)}) collective-permute-start(bf16[32,1024]{1,0:T(8,128)(2,1)S(1)} %dynamic-slice_bitcast_fusion.h.h0), channel_id=1, source_target_pairs={{0,3},{1,0},{2,1},{3,2},{4,7},{5,4},{6,5},{7,6},{8,11},{9,8},{10,9... | collective-permute-start | bytes 196616 | tf_op jit(solution)/shard_map/ppermute | solution.py:198
  28.7 6.0 %collective-permute-start.1 = (bf16[32,1024]{1,0:T(8,128)(2,1)S(1)}, bf16[32,1024]{1,0:T(8,128)(2,1)S(1)}, u32[]{:S(2)}, u32[]{:S(2)}) collective-permute-start(bf16[32,1024]{1,0:T(8,128)(2,1)S(1)} %dynamic-slice_bitcast_fusion.h.h0), channel_id=1, source_target_pairs={{0,2},{1,3},{2,0},{3,1},{4,6},{5,7},{6,4},{7,5},{8,10},{9,11},{10,... | collective-permute-start | bytes 196616 | tf_op jit(solution)/shard_map/ppermute | solution.py:198
  29.5 5.7 %collective-permute-start = (bf16[32,1024]{1,0:T(8,128)(2,1)S(1)}, bf16[32,1024]{1,0:T(8,128)(2,1)S(1)}, u32[]{:S(2)}, u32[]{:S(2)}) collective-permute-start(bf16[32,1024]{1,0:T(8,128)(2,1)S(1)} %dynamic-slice_bitcast_fusion.h.h0), channel_id=1, source_target_pairs={{0,1},{1,2},{2,3},{3,0},{4,5},{5,6},{6,7},{7,4},{8,9},{9,10},{10,1... | collective-permute-start | bytes 196616 | tf_op jit(solution)/shard_map/ppermute | solution.py:198
  30.4 4.8 %copy-start = (bf16[4096,1024]{1,0:T(8,128)(2,1)S(1)}, bf16[4096,1024]{1,0:T(8,128)(2,1)}, u32[]{:S(2)}) copy-start(bf16[4096,1024]{1,0:T(8,128)(2,1)} %wq.1) | copy-start | bytes 25165828
  32.5 2.0 %copy-start.2 = (bf16[4096,256]{1,0:T(8,128)(2,1)S(1)}, bf16[4096,256]{1,0:T(8,128)(2,1)}, u32[]{:S(2)}) copy-start(bf16[4096,256]{1,0:T(8,128)(2,1)} %wv.3) | copy-start | bytes 6291460
  34.4 49.3 %slice-start = ((s8[8388608]{0:T(1024)(128)(4,1)}), s8[4194304]{0:T(1024)(128)(4,1)S(1)}, s32[]{:S(2)}) async-start(s8[8388608]{0:T(1024)(128)(4,1)} %bitcast.15), calls=%async_computation.3 | async-start | bytes 8388608
  35.2 48.6 %slice-start.1 = ((s8[8388608]{0:T(1024)(128)(4,1)}), s8[4194304]{0:T(1024)(128)(4,1)S(1)}, s32[]{:S(2)}) async-start(s8[8388608]{0:T(1024)(128)(4,1)} %bitcast.15), calls=%async_computation.4 | async-start | bytes 8388608
  85.9 5.9 %collective-permute-start.3 = (bf16[32,1024]{1,0:T(8,128)(2,1)S(1)}, bf16[32,1024]{1,0:T(8,128)(2,1)S(1)}, u32[]{:S(2)}, u32[]{:S(2)}) collective-permute-start(bf16[32,1024]{1,0:T(8,128)(2,1)S(1)} %get-tuple-element.42), channel_id=1, source_target_pairs={{0,2},{1,3},{2,0},{3,1},{4,6},{5,7},{6,4},{7,5},{8,10},{9,11},{10,... | collective-permute-start | bytes 196616 | tf_op jit(solution)/shard_map/ppermute | solution.py:198
  88.5 5.5 %collective-permute-start.4 = (bf16[32,1024]{1,0:T(8,128)(2,1)S(1)}, bf16[32,1024]{1,0:T(8,128)(2,1)S(1)}, u32[]{:S(2)}, u32[]{:S(2)}) collective-permute-start(bf16[32,1024]{1,0:T(8,128)(2,1)S(1)} %get-tuple-element.43), channel_id=1, source_target_pairs={{0,1},{1,2},{2,3},{3,0},{4,5},{5,6},{6,7},{7,4},{8,9},{9,10},{10,1... | collective-permute-start | bytes 196616 | tf_op jit(solution)/shard_map/ppermute | solution.py:198
  89.3 4.7 %collective-permute-start.5 = (bf16[32,1024]{1,0:T(8,128)(2,1)S(1)}, bf16[32,1024]{1,0:T(8,128)(2,1)S(1)}, u32[]{:S(2)}, u32[]{:S(2)}) collective-permute-start(bf16[32,1024]{1,0:T(8,128)(2,1)S(1)} %get-tuple-element.44), channel_id=1, source_target_pairs={{0,3},{1,0},{2,1},{3,2},{4,7},{5,4},{6,5},{7,6},{8,11},{9,8},{10,9... | collective-permute-start | bytes 196616 | tf_op jit(solution)/shard_map/ppermute | solution.py:198

commit v5 on v4

--- a/solution.py
+++ b/solution.py
@@ -87,14 +87,10 @@
     lane = lax.broadcasted_iota(jnp.int32, (rows, HEAD), 1)
     key_at = lax.broadcasted_iota(jnp.int32, (groups * rows, share), 1) + lax.axis_index("ctx") * share
     row_at = lax.rem(lax.broadcasted_iota(jnp.int32, (groups * rows, share), 0), rows)
-    ones = (lax.broadcasted_iota(jnp.int32, (share, HEAD), 1) == 0).astype(bf16)
+    ones = jnp.ones((share, HEAD), bf16)
     chunk_at = lax.broadcasted_iota(jnp.int32, (chunk, HEAD), 0)
-    chunk_lane = lax.broadcasted_iota(jnp.int32, (chunk, HEAD), 1)
-    counted = [
-        jnp.where((chunk_at < len_ref[0] - c) & (chunk_lane == 0), 1.0, 0.0).astype(bf16) for c in starts
-    ]
-    hidden = [jnp.where(chunk_at < len_ref[0] - c, 0.0, 1.0).astype(bf16) for c in starts]
-    fill = [[gone * k[kv, 0:1, :] for gone in hidden] for kv in range(2)]
+    counted = [jnp.where(chunk_at < len_ref[0] - c, 1.0, 0.0).astype(bf16) for c in starts]
+    fill = [[(1 - count) * k[kv, 0:1, :] for count in counted] for kv in range(2)]
 
     def keys_of(kv, n):
         block = k[kv, n * chunk : (n + 1) * chunk, :]
@@ -132,7 +128,7 @@
             part = acc[g * rows : (g + 1) * rows]
             out[r : r + rows, h * HEAD : (h + 1) * HEAD] = part[:, :HEAD].astype(bf16)
             tops_at = jnp.where(lane == h, top[g * rows : (g + 1) * rows], tops_at)
-            sums_at = jnp.where(lane == h, part[:, HEAD : HEAD + 1], sums_at)
+            sums_at = jnp.where(lane == h, part[:, HEAD:], sums_at)
         if kv == 1:
             fields = split3(tops_at) + split3(sums_at)
             side = fields[0] + sum(pltpu.roll(x, 8 * f, 1) for f, x in enumerate(fields) if f)

time: 95.3 us -> 95.2 us (level)
  no operation moved by 1% of the time
where the time goes in v5:
time: 95.2 us; the launch traced here: 94.5 us
  blocking collectives  35.6 us (37%)
  waiting for transfers between devices  19.1 us (20%)
  starting transfers between devices  18.6 us (20%)
  Pallas kernels  15.2 us (16%)
  other arithmetic  2.71 us (3%)
  local copies, waits for them, and re-layouts  1.98 us (2%)
  between operations  1.38 us (1%)
    all_to_all x1, blocking collectives, local(): parts = lax.all_to_all(sent.reshape(CTX, share, -1), 'ctx', 0, 0)  17.9 us
    all_to_all x1, blocking collectives, local(): queries = lax.all_to_all(queries, 'ctx', 0, 0).reshape(count, -1)  17.7 us
    all_to_all x1, waiting for transfers between devices, local(): chunks = lax.all_to_all(response[0].reshape(CTX, share, feats), 'ctx', 0, 0)  16.4 us
    pallas_call x1, Pallas kernels, attend(): pl.pallas_call(functools.partial(attend_kernel, rows=rows, chunk=chunk),...  10.7 us
    ppermute x6, starting transfers between devices, shift(): return lax.ppermute(x, 'tp', [(i, (i + s) % TP) for i in range(TP)])  10.3 us
    all_to_all x1, starting transfers between devices, local(): chunks = lax.all_to_all(response[0].reshape(CTX, share, feats), 'ctx', 0, 0)  8.26 us
    ppermute x6, waiting for transfers between devices, shift(): return lax.ppermute(x, 'tp', [(i, (i + s) % TP) for i in range(TP)])  2.71 us
    pallas_call x1, Pallas kernels, project(): pl.pallas_call(project_kernel, in_specs=[vmem] * 9, out_specs=[vmem] * 3,...  2.11 us
  transfers between devices with their start and end apart: 7, of which 3 were waited for; matrix products, arithmetic and copies ran while one was open for 2% of the time, Pallas kernels for 0%

profile of v5, /device:TPU:0, one launch (start us, length us, event | category | flops | bytes accessed | tf_op | source)
XLA Modules:
  0.0 94.5 jit_solution(8617402115059188509)
XLA Ops:
  0.0 0.0 copy-start.1
  0.0 8.3 %all-to-all-start = ((bf16[16,32,1024]{2,1,0:T(8,128)(2,1)}), bf16[16,32,1024]{2,1,0:T(8,128)(2,1)S(1)}, u32[]{:S(2)}, u32[]{:S(2)}) async-start(bf16[16,32,1024]{2,1,0:T(8,128)(2,1)} %bitcast.19), calls=%async_computation | async-start | bytes 2097152 | tf_op jit(solution)/shard_map/all_to_all | solution.py:201
  9.6 16.4 %all-to-all-done = bf16[16,32,1024]{2,1,0:T(8,128)(2,1)S(1)} async-done(((bf16[16,32,1024]{2,1,0:T(8,128)(2,1)}), bf16[16,32,1024]{2,1,0:T(8,128)(2,1)S(1)}, u32[]{:S(2)}, u32[]{:S(2)}) %all-to-all-start) | async-done | bytes 1048608 | tf_op jit(solution)/shard_map/all_to_all | solution.py:201
  26.0 2.8 %collective-permute-start.2 = (bf16[32,1024]{1,0:T(8,128)(2,1)S(1)}, bf16[32,1024]{1,0:T(8,128)(2,1)S(1)}, u32[]{:S(2)}, u32[]{:S(2)}) collective-permute-start(bf16[32,1024]{1,0:T(8,128)(2,1)S(1)} %dynamic-slice_bitcast_fusion.h.h0), channel_id=1, source_target_pairs={{0,3},{1,0},{2,1},{3,2},{4,7},{5,4},{6,5},{7,6},{8,11},{9,8},{10,9... | collective-permute-start | bytes 196616 | tf_op jit(solution)/shard_map/ppermute | solution.py:194
  28.7 0.8 collective-permute-start.1
  29.5 0.9 collective-permute-start
  30.4 0.0 copy-start
  30.4 2.0 %fusion = (bf16[2,2048,128]{2,1,0:T(8,128)(2,1)S(1)}, bf16[2,2048,128]{2,1,0:T(8,128)(2,1)S(1)}) fusion(bf16[2048,2,128]{2,1,0:T(2,128)(2,1)} %param.13, pred[2048]{0:T(1024)(128)(4,1)S(1)} %iota_compare_fusion, bf16[2048,2,128]{2,1,0:T(2,128)(2,1)} %param.12), kind=kLoop, calls=%fused_computation.1 | loop fusion | flops 1048576 | bytes 4196352 | tf_op jit(solution)/shard_map/transpose | solution.py:209
  32.5 0.0 copy-done.1
  32.5 0.0 copy-start.2
  32.5 2.0 %copy-done.2 = bf16[4096,256]{1,0:T(8,128)(2,1)S(1)} copy-done((bf16[4096,256]{1,0:T(8,128)(2,1)S(1)}, bf16[4096,256]{1,0:T(8,128)(2,1)}, u32[]{:S(2)}) %copy-start.2) | copy-done | bytes 2097176
  34.4 0.0 slice-start
  34.5 0.3 shard_map.91
  34.7 0.0 collective-permute-done.2.h3
  34.7 0.0 collective-permute-done.1.h2
  34.8 0.5 collective-permute-done.h1
  35.2 0.0 copy-done
  35.2 0.0 slice-start.1
  35.2 2.1 %shard_map.92 = (bf16[16,32,1024]{2,1,0:T(8,128)(2,1)S(1)}, bf16[32,256]{1,0:T(8,128)(2,1)S(1)}, bf16[32,256]{1,0:T(8,128)(2,1)S(1)}) custom-call(bf16[32,1024]{1,0:T(8,128)(2,1)S(1)} %dynamic-slice_bitcast_fusion.h.h0, bf16[32,1024]{1,0:T(8,128)(2,1)S(1)} %collective-permute-done.h1, bf16[32,1024]{1,0:T(8,128)(2,1)S(1)} %collective-permute-done.1.h2, ...), custom_call_target="tpu_custom_call" | custom-call | tf_op jit(solution)/shard_map/pallas_call | solution.py:65
  37.3 17.7 %all_to_all.15 = bf16[16,32,1024]{2,1,0:T(8,128)(2,1)S(1)} all-to-all(bf16[16,32,1024]{2,1,0:T(8,128)(2,1)S(1)} %get-tuple-element.36), channel_id=1, replica_groups=mesh['dp'=2,'ctx'=16,'tp'=4] {'ctx'}, dimensions={0} | all-to-all | bytes 2097152 | tf_op jit(solution)/shard_map/all_to_all | solution.py:215
  55.0 10.7 %shard_map.93 = bf16[512,1152]{1,0:T(8,128)(2,1)S(1)} custom-call(s32[1]{0:T(128)} %copy.19.len_ref, bf16[512,1024]{1,0:T(8,128)(2,1)S(1)} %bitcast.18, bf16[2,2048,128]{2,1,0:T(8,128)(2,1)S(1)} %get-tuple-element.37.ready.k, bf16[2,2048,128]{2,1,0:T(8,128)(2,1)S(1)} %get-tuple-element.38.v, bf16[32,256]{1,0:T(8,128)(2,1)S(1)} %get-tuple-element.39.ks, ...), custom_call_target="tpu_custom_call" | custom-call | bytes 33554432 | tf_op jit(solution)/shard_map/pallas_call | solution.py:142
  65.7 17.9 %all_to_all.16.parts = bf16[16,32,1152]{2,1,0:T(8,128)(2,1)S(1)} all-to-all(bf16[16,32,1152]{2,1,0:T(8,128)(2,1)S(1)} %bitcast.17), channel_id=1, replica_groups=mesh['dp'=2,'ctx'=16,'tp'=4] {'ctx'}, dimensions={0} | all-to-all | bytes 2359296 | tf_op jit(solution)/shard_map/all_to_all | solution.py:217
  83.7 0.0 slice-done
  83.7 0.0 slice-done.1
  83.7 2.1 %shard_map.94 = (bf16[32,1024]{1,0:T(8,128)(2,1)S(1)}, bf16[32,1024]{1,0:T(8,128)(2,1)S(1)}, bf16[32,1024]{1,0:T(8,128)(2,1)S(1)}, bf16[32,1024]{1,0:T(8,128)(2,1)S(1)}) custom-call(bf16[16,32,1152]{2,1,0:T(8,128)(2,1)S(1)} %all_to_all.16.parts, bf16[1024,4096]{1,0:T(8,128)(2,1)S(1)} %bitcast.16), custom_call_target="tpu_custom_call" | custom-call | flops 268435456 | bytes 8388608 | tf_op jit(solution)/shard_map/pallas_call | solution.py:181
  85.8 2.6 %collective-permute-start.3 = (bf16[32,1024]{1,0:T(8,128)(2,1)S(1)}, bf16[32,1024]{1,0:T(8,128)(2,1)S(1)}, u32[]{:S(2)}, u32[]{:S(2)}) collective-permute-start(bf16[32,1024]{1,0:T(8,128)(2,1)S(1)} %get-tuple-element.42), channel_id=1, source_target_pairs={{0,2},{1,3},{2,0},{3,1},{4,6},{5,7},{6,4},{7,5},{8,10},{9,11},{10,... | collective-permute-start | bytes 196616 | tf_op jit(solution)/shard_map/ppermute | solution.py:194
  88.4 0.8 collective-permute-start.4
  89.2 2.4 %collective-permute-start.5 = (bf16[32,1024]{1,0:T(8,128)(2,1)S(1)}, bf16[32,1024]{1,0:T(8,128)(2,1)S(1)}, u32[]{:S(2)}, u32[]{:S(2)}) collective-permute-start(bf16[32,1024]{1,0:T(8,128)(2,1)S(1)} %get-tuple-element.44), channel_id=1, source_target_pairs={{0,3},{1,0},{2,1},{3,2},{4,7},{5,4},{6,5},{7,6},{8,11},{9,8},{10,9... | collective-permute-start | bytes 196616 | tf_op jit(solution)/shard_map/ppermute | solution.py:194
  91.6 0.0 collective-permute-done.3
  91.6 2.2 %collective-permute-done.4 = bf16[32,1024]{1,0:T(8,128)(2,1)S(1)} collective-permute-done((bf16[32,1024]{1,0:T(8,128)(2,1)S(1)}, bf16[32,1024]{1,0:T(8,128)(2,1)S(1)}, u32[]{:S(2)}, u32[]{:S(2)}) %collective-permute-start.4) | collective-permute-done | bytes 65568 | tf_op jit(solution)/shard_map/ppermute | solution.py:194
  93.9 0.0 collective-permute-done.5
  93.9 0.7 add_convert_fusion
  (3 shorter events, 0.0 us)
Async XLA Ops:
  0.0 32.5 %copy-start.1 = (bf16[4096,256]{1,0:T(8,128)(2,1)S(1)}, bf16[4096,256]{1,0:T(8,128)(2,1)}, u32[]{:S(2)}) copy-start(bf16[4096,256]{1,0:T(8,128)(2,1)} %wk.3) | copy-start | bytes 6291460
  0.0 26.0 %all-to-all-start = ((bf16[16,32,1024]{2,1,0:T(8,128)(2,1)}), bf16[16,32,1024]{2,1,0:T(8,128)(2,1)S(1)}, u32[]{:S(2)}, u32[]{:S(2)}) async-start(bf16[16,32,1024]{2,1,0:T(8,128)(2,1)} %bitcast.19), calls=%async_computation | async-start | bytes 2097152 | tf_op jit(solution)/shard_map/all_to_all | solution.py:201
  26.0 8.8 %collective-permute-start.2 = (bf16[32,1024]{1,0:T(8,128)(2,1)S(1)}, bf16[32,1024]{1,0:T(8,128)(2,1)S(1)}, u32[]{:S(2)}, u32[]{:S(2)}) collective-permute-start(bf16[32,1024]{1,0:T(8,128)(2,1)S(1)} %dynamic-slice_bitcast_fusion.h.h0), channel_id=1, source_target_pairs={{0,3},{1,0},{2,1},{3,2},{4,7},{5,4},{6,5},{7,6},{8,11},{9,8},{10,9... | collective-permute-start | bytes 196616 | tf_op jit(solution)/shard_map/ppermute | solution.py:194
  28.7 6.0 %collective-permute-start.1 = (bf16[32,1024]{1,0:T(8,128)(2,1)S(1)}, bf16[32,1024]{1,0:T(8,128)(2,1)S(1)}, u32[]{:S(2)}, u32[]{:S(2)}) collective-permute-start(bf16[32,1024]{1,0:T(8,128)(2,1)S(1)} %dynamic-slice_bitcast_fusion.h.h0), channel_id=1, source_target_pairs={{0,2},{1,3},{2,0},{3,1},{4,6},{5,7},{6,4},{7,5},{8,10},{9,11},{10,... | collective-permute-start | bytes 196616 | tf_op jit(solution)/shard_map/ppermute | solution.py:194
  29.5 5.7 %collective-permute-start = (bf16[32,1024]{1,0:T(8,128)(2,1)S(1)}, bf16[32,1024]{1,0:T(8,128)(2,1)S(1)}, u32[]{:S(2)}, u32[]{:S(2)}) collective-permute-start(bf16[32,1024]{1,0:T(8,128)(2,1)S(1)} %dynamic-slice_bitcast_fusion.h.h0), channel_id=1, source_target_pairs={{0,1},{1,2},{2,3},{3,0},{4,5},{5,6},{6,7},{7,4},{8,9},{9,10},{10,1... | collective-permute-start | bytes 196616 | tf_op jit(solution)/shard_map/ppermute | solution.py:194
  30.4 4.8 %copy-start = (bf16[4096,1024]{1,0:T(8,128)(2,1)S(1)}, bf16[4096,1024]{1,0:T(8,128)(2,1)}, u32[]{:S(2)}) copy-start(bf16[4096,1024]{1,0:T(8,128)(2,1)} %wq.1) | copy-start | bytes 25165828
  32.5 2.0 %copy-start.2 = (bf16[4096,256]{1,0:T(8,128)(2,1)S(1)}, bf16[4096,256]{1,0:T(8,128)(2,1)}, u32[]{:S(2)}) copy-start(bf16[4096,256]{1,0:T(8,128)(2,1)} %wv.3) | copy-start | bytes 6291460
  34.4 49.2 %slice-start = ((s8[8388608]{0:T(1024)(128)(4,1)}), s8[4194304]{0:T(1024)(128)(4,1)S(1)}, s32[]{:S(2)}) async-start(s8[8388608]{0:T(1024)(128)(4,1)} %bitcast.15), calls=%async_computation.3 | async-start | bytes 8388608
  35.2 48.5 %slice-start.1 = ((s8[8388608]{0:T(1024)(128)(4,1)}), s8[4194304]{0:T(1024)(128)(4,1)S(1)}, s32[]{:S(2)}) async-start(s8[8388608]{0:T(1024)(128)(4,1)} %bitcast.15), calls=%async_computation.4 | async-start | bytes 8388608
  85.8 5.9 %collective-permute-start.3 = (bf16[32,1024]{1,0:T(8,128)(2,1)S(1)}, bf16[32,1024]{1,0:T(8,128)(2,1)S(1)}, u32[]{:S(2)}, u32[]{:S(2)}) collective-permute-start(bf16[32,1024]{1,0:T(8,128)(2,1)S(1)} %get-tuple-element.42), channel_id=1, source_target_pairs={{0,2},{1,3},{2,0},{3,1},{4,6},{5,7},{6,4},{7,5},{8,10},{9,11},{10,... | collective-permute-start | bytes 196616 | tf_op jit(solution)/shard_map/ppermute | solution.py:194
  88.4 5.5 %collective-permute-start.4 = (bf16[32,1024]{1,0:T(8,128)(2,1)S(1)}, bf16[32,1024]{1,0:T(8,128)(2,1)S(1)}, u32[]{:S(2)}, u32[]{:S(2)}) collective-permute-start(bf16[32,1024]{1,0:T(8,128)(2,1)S(1)} %get-tuple-element.43), channel_id=1, source_target_pairs={{0,1},{1,2},{2,3},{3,0},{4,5},{5,6},{6,7},{7,4},{8,9},{9,10},{10,1... | collective-permute-start | bytes 196616 | tf_op jit(solution)/shard_map/ppermute | solution.py:194
  89.2 4.7 %collective-permute-start.5 = (bf16[32,1024]{1,0:T(8,128)(2,1)S(1)}, bf16[32,1024]{1,0:T(8,128)(2,1)S(1)}, u32[]{:S(2)}, u32[]{:S(2)}) collective-permute-start(bf16[32,1024]{1,0:T(8,128)(2,1)S(1)} %get-tuple-element.44), channel_id=1, source_target_pairs={{0,3},{1,0},{2,1},{3,2},{4,7},{5,4},{6,5},{7,6},{8,11},{9,8},{10,9... | collective-permute-start | bytes 196616 | tf_op jit(solution)/shard_map/ppermute | solution.py:194

commit v6 on v5

--- a/solution.py
+++ b/solution.py
@@ -44,18 +44,16 @@
 
 def project_kernel(h0, h1, h2, h3, k0, v0, wq, wk, wv, queries, keys, values):
     feats = h0.shape[1]
-    totals = [0.0, k0[...], v0[...]]
-    for s, h in enumerate((h0, h1, h2, h3)):
-        start = pl.multiple_of(lax.rem(lax.axis_index("tp") + TP - s, TP) * feats, feats)
-        rows = h[...]
-        for m, w in enumerate((wq, wk, wv)):
-            if s > 0 or m == 0:
-                totals[m] = totals[m] + dot(rows, w[pl.ds(start, feats), :])
-    q = totals[0].astype(bf16)
+    starts = [pl.multiple_of(lax.rem(lax.axis_index("tp") + TP - s, TP) * feats, feats) for s in range(TP)]
+    pieces = [h[...] for h in (h0, h1, h2, h3)]
+    q = sum(dot(h, wq[pl.ds(c, feats), :]) for h, c in zip(pieces, starts)).astype(bf16)
     for c in range(CTX):
         queries[c] = q
-    keys[...] = totals[1].astype(bf16)
-    values[...] = totals[2].astype(bf16)
+    for out, begun, w in ((keys, k0, wk), (values, v0, wv)):
+        total = begun[...]
+        for h, c in zip(pieces[1:], starts[1:]):
+            total = total + dot(h, w[pl.ds(c, feats), :])
+        out[...] = total.astype(bf16)
 
 
 def project(pieces, begun, w_query, w_key, w_value):

time: 95.2 us -> 95.2 us (level)
  no operation moved by 1% of the time
where the time goes in v6:
time: 95.2 us; the launch traced here: 94.5 us
  blocking collectives  35.6 us (37%)
  waiting for transfers between devices  19.1 us (20%)
  starting transfers between devices  18.6 us (20%)
  Pallas kernels  15.2 us (16%)
  other arithmetic  2.71 us (3%)
  local copies, waits for them, and re-layouts  1.98 us (2%)
  between operations  1.37 us (1%)
    all_to_all x1, blocking collectives, local(): parts = lax.all_to_all(sent.reshape(CTX, share, -1), 'ctx', 0, 0)  17.9 us
    all_to_all x1, blocking collectives, local(): queries = lax.all_to_all(queries, 'ctx', 0, 0).reshape(count, -1)  17.7 us
    all_to_all x1, waiting for transfers between devices, local(): chunks = lax.all_to_all(response[0].reshape(CTX, share, feats), 'ctx', 0, 0)  16.4 us
    pallas_call x1, Pallas kernels, attend(): pl.pallas_call(functools.partial(attend_kernel, rows=rows, chunk=chunk),...  10.7 us
    ppermute x6, starting transfers between devices, shift(): return lax.ppermute(x, 'tp', [(i, (i + s) % TP) for i in range(TP)])  10.3 us
    all_to_all x1, starting transfers between devices, local(): chunks = lax.all_to_all(response[0].reshape(CTX, share, feats), 'ctx', 0, 0)  8.26 us
    ppermute x6, waiting for transfers between devices, shift(): return lax.ppermute(x, 'tp', [(i, (i + s) % TP) for i in range(TP)])  2.71 us
    pallas_call x1, Pallas kernels, project(): pl.pallas_call(project_kernel, in_specs=[vmem] * 9, out_specs=[vmem] * 3,...  2.12 us
  transfers between devices with their start and end apart: 7, of which 3 were waited for; matrix products, arithmetic and copies ran while one was open for 2% of the time, Pallas kernels for 0%

profile of v6, /device:TPU:0, one launch (start us, length us, event | category | flops | bytes accessed | tf_op | source)
XLA Modules:
  0.0 94.5 jit_solution(15370282022352376575)
XLA Ops:
  0.0 0.0 copy-start.1
  0.0 8.3 %all-to-all-start = ((bf16[16,32,1024]{2,1,0:T(8,128)(2,1)}), bf16[16,32,1024]{2,1,0:T(8,128)(2,1)S(1)}, u32[]{:S(2)}, u32[]{:S(2)}) async-start(bf16[16,32,1024]{2,1,0:T(8,128)(2,1)} %bitcast.19), calls=%async_computation | async-start | bytes 2097152 | tf_op jit(solution)/shard_map/all_to_all | solution.py:199
  9.6 16.4 %all-to-all-done = bf16[16,32,1024]{2,1,0:T(8,128)(2,1)S(1)} async-done(((bf16[16,32,1024]{2,1,0:T(8,128)(2,1)}), bf16[16,32,1024]{2,1,0:T(8,128)(2,1)S(1)}, u32[]{:S(2)}, u32[]{:S(2)}) %all-to-all-start) | async-done | bytes 1048608 | tf_op jit(solution)/shard_map/all_to_all | solution.py:199
  26.0 2.8 %collective-permute-start.2 = (bf16[32,1024]{1,0:T(8,128)(2,1)S(1)}, bf16[32,1024]{1,0:T(8,128)(2,1)S(1)}, u32[]{:S(2)}, u32[]{:S(2)}) collective-permute-start(bf16[32,1024]{1,0:T(8,128)(2,1)S(1)} %dynamic-slice_bitcast_fusion.h.h0), channel_id=1, source_target_pairs={{0,3},{1,0},{2,1},{3,2},{4,7},{5,4},{6,5},{7,6},{8,11},{9,8},{10,9... | collective-permute-start | bytes 196616 | tf_op jit(solution)/shard_map/ppermute | solution.py:192
  28.7 0.8 collective-permute-start.1
  29.5 0.9 collective-permute-start
  30.4 0.0 copy-start
  30.4 2.0 %fusion = (bf16[2,2048,128]{2,1,0:T(8,128)(2,1)S(1)}, bf16[2,2048,128]{2,1,0:T(8,128)(2,1)S(1)}) fusion(bf16[2048,2,128]{2,1,0:T(2,128)(2,1)} %param.13, pred[2048]{0:T(1024)(128)(4,1)S(1)} %iota_compare_fusion, bf16[2048,2,128]{2,1,0:T(2,128)(2,1)} %param.12), kind=kLoop, calls=%fused_computation.1 | loop fusion | flops 1048576 | bytes 4196352 | tf_op jit(solution)/shard_map/transpose | solution.py:207
  32.5 0.0 copy-done.1
  32.5 0.0 copy-start.2
  32.5 2.0 %copy-done.2 = bf16[4096,256]{1,0:T(8,128)(2,1)S(1)} copy-done((bf16[4096,256]{1,0:T(8,128)(2,1)S(1)}, bf16[4096,256]{1,0:T(8,128)(2,1)}, u32[]{:S(2)}) %copy-start.2) | copy-done | bytes 2097176
  34.4 0.0 slice-start
  34.5 0.3 shard_map.91
  34.7 0.0 collective-permute-done.2.h3
  34.7 0.0 collective-permute-done.1.h2
  34.8 0.5 collective-permute-done.h1
  35.2 0.0 copy-done
  35.2 0.0 slice-start.1
  35.2 2.1 %shard_map.92 = (bf16[16,32,1024]{2,1,0:T(8,128)(2,1)S(1)}, bf16[32,256]{1,0:T(8,128)(2,1)S(1)}, bf16[32,256]{1,0:T(8,128)(2,1)S(1)}) custom-call(bf16[32,1024]{1,0:T(8,128)(2,1)S(1)} %dynamic-slice_bitcast_fusion.h.h0, bf16[32,1024]{1,0:T(8,128)(2,1)S(1)} %collective-permute-done.h1, bf16[32,1024]{1,0:T(8,128)(2,1)S(1)} %collective-permute-done.1.h2, ...), custom_call_target="tpu_custom_call" | custom-call | tf_op jit(solution)/shard_map/pallas_call | solution.py:63
  37.3 17.7 %all_to_all.15 = bf16[16,32,1024]{2,1,0:T(8,128)(2,1)S(1)} all-to-all(bf16[16,32,1024]{2,1,0:T(8,128)(2,1)S(1)} %get-tuple-element.36), channel_id=1, replica_groups=mesh['dp'=2,'ctx'=16,'tp'=4] {'ctx'}, dimensions={0} | all-to-all | bytes 2097152 | tf_op jit(solution)/shard_map/all_to_all | solution.py:213
  55.0 10.7 %shard_map.93 = bf16[512,1152]{1,0:T(8,128)(2,1)S(1)} custom-call(s32[1]{0:T(128)} %copy.19.len_ref, bf16[512,1024]{1,0:T(8,128)(2,1)S(1)} %bitcast.18, bf16[2,2048,128]{2,1,0:T(8,128)(2,1)S(1)} %get-tuple-element.37.ready.k, bf16[2,2048,128]{2,1,0:T(8,128)(2,1)S(1)} %get-tuple-element.38.v, bf16[32,256]{1,0:T(8,128)(2,1)S(1)} %get-tuple-element.39.ks, ...), custom_call_target="tpu_custom_call" | custom-call | bytes 33554432 | tf_op jit(solution)/shard_map/pallas_call | solution.py:140
  65.7 17.9 %all_to_all.16.parts = bf16[16,32,1152]{2,1,0:T(8,128)(2,1)S(1)} all-to-all(bf16[16,32,1152]{2,1,0:T(8,128)(2,1)S(1)} %bitcast.17), channel_id=1, replica_groups=mesh['dp'=2,'ctx'=16,'tp'=4] {'ctx'}, dimensions={0} | all-to-all | bytes 2359296 | tf_op jit(solution)/shard_map/all_to_all | solution.py:215
  83.7 0.0 slice-done
  83.7 0.0 slice-done.1
  83.7 2.1 %shard_map.94 = (bf16[32,1024]{1,0:T(8,128)(2,1)S(1)}, bf16[32,1024]{1,0:T(8,128)(2,1)S(1)}, bf16[32,1024]{1,0:T(8,128)(2,1)S(1)}, bf16[32,1024]{1,0:T(8,128)(2,1)S(1)}) custom-call(bf16[16,32,1152]{2,1,0:T(8,128)(2,1)S(1)} %all_to_all.16.parts, bf16[1024,4096]{1,0:T(8,128)(2,1)S(1)} %bitcast.16), custom_call_target="tpu_custom_call" | custom-call | flops 268435456 | bytes 8388608 | tf_op jit(solution)/shard_map/pallas_call | solution.py:179
  85.7 2.6 %collective-permute-start.3 = (bf16[32,1024]{1,0:T(8,128)(2,1)S(1)}, bf16[32,1024]{1,0:T(8,128)(2,1)S(1)}, u32[]{:S(2)}, u32[]{:S(2)}) collective-permute-start(bf16[32,1024]{1,0:T(8,128)(2,1)S(1)} %get-tuple-element.42), channel_id=1, source_target_pairs={{0,2},{1,3},{2,0},{3,1},{4,6},{5,7},{6,4},{7,5},{8,10},{9,11},{10,... | collective-permute-start | bytes 196616 | tf_op jit(solution)/shard_map/ppermute | solution.py:192
  88.4 0.8 collective-permute-start.4
  89.2 2.4 %collective-permute-start.5 = (bf16[32,1024]{1,0:T(8,128)(2,1)S(1)}, bf16[32,1024]{1,0:T(8,128)(2,1)S(1)}, u32[]{:S(2)}, u32[]{:S(2)}) collective-permute-start(bf16[32,1024]{1,0:T(8,128)(2,1)S(1)} %get-tuple-element.44), channel_id=1, source_target_pairs={{0,3},{1,0},{2,1},{3,2},{4,7},{5,4},{6,5},{7,6},{8,11},{9,8},{10,9... | collective-permute-start | bytes 196616 | tf_op jit(solution)/shard_map/ppermute | solution.py:192
  91.6 0.0 collective-permute-done.3
  91.6 2.2 %collective-permute-done.4 = bf16[32,1024]{1,0:T(8,128)(2,1)S(1)} collective-permute-done((bf16[32,1024]{1,0:T(8,128)(2,1)S(1)}, bf16[32,1024]{1,0:T(8,128)(2,1)S(1)}, u32[]{:S(2)}, u32[]{:S(2)}) %collective-permute-start.4) | collective-permute-done | bytes 65568 | tf_op jit(solution)/shard_map/ppermute | solution.py:192
  93.9 0.0 collective-permute-done.5
  93.9 0.7 add_convert_fusion
  (3 shorter events, 0.0 us)
Async XLA Ops:
  0.0 32.5 %copy-start.1 = (bf16[4096,256]{1,0:T(8,128)(2,1)S(1)}, bf16[4096,256]{1,0:T(8,128)(2,1)}, u32[]{:S(2)}) copy-start(bf16[4096,256]{1,0:T(8,128)(2,1)} %wk.3) | copy-start | bytes 6291460
  0.0 26.0 %all-to-all-start = ((bf16[16,32,1024]{2,1,0:T(8,128)(2,1)}), bf16[16,32,1024]{2,1,0:T(8,128)(2,1)S(1)}, u32[]{:S(2)}, u32[]{:S(2)}) async-start(bf16[16,32,1024]{2,1,0:T(8,128)(2,1)} %bitcast.19), calls=%async_computation | async-start | bytes 2097152 | tf_op jit(solution)/shard_map/all_to_all | solution.py:199
  26.0 8.8 %collective-permute-start.2 = (bf16[32,1024]{1,0:T(8,128)(2,1)S(1)}, bf16[32,1024]{1,0:T(8,128)(2,1)S(1)}, u32[]{:S(2)}, u32[]{:S(2)}) collective-permute-start(bf16[32,1024]{1,0:T(8,128)(2,1)S(1)} %dynamic-slice_bitcast_fusion.h.h0), channel_id=1, source_target_pairs={{0,3},{1,0},{2,1},{3,2},{4,7},{5,4},{6,5},{7,6},{8,11},{9,8},{10,9... | collective-permute-start | bytes 196616 | tf_op jit(solution)/shard_map/ppermute | solution.py:192
  28.7 6.0 %collective-permute-start.1 = (bf16[32,1024]{1,0:T(8,128)(2,1)S(1)}, bf16[32,1024]{1,0:T(8,128)(2,1)S(1)}, u32[]{:S(2)}, u32[]{:S(2)}) collective-permute-start(bf16[32,1024]{1,0:T(8,128)(2,1)S(1)} %dynamic-slice_bitcast_fusion.h.h0), channel_id=1, source_target_pairs={{0,2},{1,3},{2,0},{3,1},{4,6},{5,7},{6,4},{7,5},{8,10},{9,11},{10,... | collective-permute-start | bytes 196616 | tf_op jit(solution)/shard_map/ppermute | solution.py:192
  29.5 5.7 %collective-permute-start = (bf16[32,1024]{1,0:T(8,128)(2,1)S(1)}, bf16[32,1024]{1,0:T(8,128)(2,1)S(1)}, u32[]{:S(2)}, u32[]{:S(2)}) collective-permute-start(bf16[32,1024]{1,0:T(8,128)(2,1)S(1)} %dynamic-slice_bitcast_fusion.h.h0), channel_id=1, source_target_pairs={{0,1},{1,2},{2,3},{3,0},{4,5},{5,6},{6,7},{7,4},{8,9},{9,10},{10,1... | collective-permute-start | bytes 196616 | tf_op jit(solution)/shard_map/ppermute | solution.py:192
  30.4 4.8 %copy-start = (bf16[4096,1024]{1,0:T(8,128)(2,1)S(1)}, bf16[4096,1024]{1,0:T(8,128)(2,1)}, u32[]{:S(2)}) copy-start(bf16[4096,1024]{1,0:T(8,128)(2,1)} %wq.1) | copy-start | bytes 25165828
  32.5 2.0 %copy-start.2 = (bf16[4096,256]{1,0:T(8,128)(2,1)S(1)}, bf16[4096,256]{1,0:T(8,128)(2,1)}, u32[]{:S(2)}) copy-start(bf16[4096,256]{1,0:T(8,128)(2,1)} %wv.3) | copy-start | bytes 6291460
  34.4 49.2 %slice-start = ((s8[8388608]{0:T(1024)(128)(4,1)}), s8[4194304]{0:T(1024)(128)(4,1)S(1)}, s32[]{:S(2)}) async-start(s8[8388608]{0:T(1024)(128)(4,1)} %bitcast.15), calls=%async_computation.3 | async-start | bytes 8388608
  35.2 48.5 %slice-start.1 = ((s8[8388608]{0:T(1024)(128)(4,1)}), s8[4194304]{0:T(1024)(128)(4,1)S(1)}, s32[]{:S(2)}) async-start(s8[8388608]{0:T(1024)(128)(4,1)} %bitcast.15), calls=%async_computation.4 | async-start | bytes 8388608
  85.7 5.9 %collective-permute-start.3 = (bf16[32,1024]{1,0:T(8,128)(2,1)S(1)}, bf16[32,1024]{1,0:T(8,128)(2,1)S(1)}, u32[]{:S(2)}, u32[]{:S(2)}) collective-permute-start(bf16[32,1024]{1,0:T(8,128)(2,1)S(1)} %get-tuple-element.42), channel_id=1, source_target_pairs={{0,2},{1,3},{2,0},{3,1},{4,6},{5,7},{6,4},{7,5},{8,10},{9,11},{10,... | collective-permute-start | bytes 196616 | tf_op jit(solution)/shard_map/ppermute | solution.py:192
  88.4 5.5 %collective-permute-start.4 = (bf16[32,1024]{1,0:T(8,128)(2,1)S(1)}, bf16[32,1024]{1,0:T(8,128)(2,1)S(1)}, u32[]{:S(2)}, u32[]{:S(2)}) collective-permute-start(bf16[32,1024]{1,0:T(8,128)(2,1)S(1)} %get-tuple-element.43), channel_id=1, source_target_pairs={{0,1},{1,2},{2,3},{3,0},{4,5},{5,6},{6,7},{7,4},{8,9},{9,10},{10,1... | collective-permute-start | bytes 196616 | tf_op jit(solution)/shard_map/ppermute | solution.py:192
  89.2 4.7 %collective-permute-start.5 = (bf16[32,1024]{1,0:T(8,128)(2,1)S(1)}, bf16[32,1024]{1,0:T(8,128)(2,1)S(1)}, u32[]{:S(2)}, u32[]{:S(2)}) collective-permute-start(bf16[32,1024]{1,0:T(8,128)(2,1)S(1)} %get-tuple-element.44), channel_id=1, source_target_pairs={{0,3},{1,0},{2,1},{3,2},{4,7},{5,4},{6,5},{7,6},{8,11},{9,8},{10,9... | collective-permute-start | bytes 196616 | tf_op jit(solution)/shard_map/ppermute | solution.py:192
